TPU v7x, 512 devices: a whole 4x4x16 slice. The times are simulated.
512 devices in a mesh: ctx: 64 (over z, x), tp: 8 (over y, core).
Axes of the slice: x: 4, y: 4, z: 16, core: 2. Of those that a mesh axis runs over, the one named last changes fastest.
Arguments:
- hidden_in: bfloat16 [64, 8192], P(None, 'ctx'), may hold values from -3 to 3
- attn_gain: float32 [8192], P('ctx'), may hold values from 0.5 to 2
- w_query: bfloat16 [8192, 8192], P('ctx', 'tp'), may hold values from -0.0625 to 0.0625
- key_cache: bfloat16 [32768, 1024], P('ctx', 'tp'), may hold values from -41 to 41
- value_cache: bfloat16 [32768, 1024], P('ctx', 'tp'), may hold values from -6 to 6
- block_lengths: int32 [64], P('ctx'), may hold values from 1 to 512, 24576 in all
- question_length: int32 [1], replicated, may hold values from 32 to 64
- w_out: bfloat16 [8192, 8192], P('tp', 'ctx'), may hold values from -0.0625 to 0.0625
- ffn_gain: float32 [8192], P('ctx'), may hold values from 0.5 to 2
- w_gate: bfloat16 [8192, 14336], P('ctx', 'tp'), may hold values from -0.0625 to 0.0625
- w_up: bfloat16 [8192, 14336], P('ctx', 'tp'), may hold values from -0.0625 to 0.0625
- w_down: bfloat16 [14336, 8192], P('tp', 'ctx'), may hold values from -0.046875 to 0.046875
Outputs:
- layer_out: bfloat16 [64, 8192], P(None, 'ctx')
Inputs may be any that keep to these rules, and one draw needn't show every extreme that they name: `block_lengths`: each block has at least one valid token, and some block is full.
All inputs are finite; a program needn't handle non-finite values.
Results may differ from a plain program's by a relative error of at most 0.012.
The roundings to bfloat16 on the way count: a program that leaves them out, or rounds other values in their place, can miss the bound.
Values may be sent and summed in bfloat16 or wider, within the bound.
A program may use at most 64 MiB of HBM per device.

v0:
```python
import math

import jax
import jax.numpy as jnp
from jax import lax
from jax.sharding import PartitionSpec as P

D = 8192
HD = 128


EPSILON = 1e-05
MASKED = -1e30


def combined_all(part, axis, combine):
    gathered = jax.tree.map(lambda a: lax.all_gather(a, axis), part)

    def take(source):
        return jax.tree.map(lambda a: lax.dynamic_index_in_dim(a, source, 0, False), gathered)

    return lax.fori_loop(
        1, lax.axis_size(axis), lambda source, state: combine(state, take(source)), take(0)
    )


def combine_pieces(first, second):
    summit = jnp.maximum(first[0], second[0])
    first_factor = jnp.exp(first[0] - summit)
    second_factor = jnp.exp(second[0] - summit)
    totals = first[1] * first_factor + second[1] * second_factor
    numerators = first[2] * first_factor[..., None] + second[2] * second_factor[..., None]
    return (summit, totals, numerators)


def body(
    hidden_in,
    attn_gain,
    w_query,
    key_cache,
    value_cache,
    block_lengths,
    question_length,
    w_out,
    ffn_gain,
    w_gate,
    w_up,
    w_down,
):
    row_count = hidden_in.shape[0]
    stream = hidden_in.astype(jnp.float32)
    square_part = jnp.sum(stream * stream, axis=1)
    first_normed = (stream * attn_gain).astype(jnp.bfloat16)
    query_part = jnp.dot(first_normed, w_query, preferred_element_type=jnp.float32)
    square_sum = lax.psum(square_part, "ctx")
    query_sum = lax.psum(query_part, "ctx")
    first_scale = lax.rsqrt(square_sum / D + EPSILON)
    queries = (first_scale[:, None] * query_sum).astype(jnp.bfloat16)
    kv_local = key_cache.shape[1] // HD
    groups = queries.shape[1] // HD // kv_local
    block_rows = key_cache.shape[0]
    query_heads = queries.reshape(row_count, kv_local, groups, HD).transpose(1, 2, 0, 3)
    key_heads = key_cache.reshape(block_rows, kv_local, HD).transpose(1, 0, 2)
    value_heads = value_cache.reshape(block_rows, kv_local, HD).transpose(1, 0, 2)
    usable = jnp.arange(block_rows) < block_lengths[0]
    score_scale = 1.0 / math.sqrt(HD)

    def one_head(operands):
        query_head, key_head, value_head = operands
        scores = (
            jnp.einsum("grd,jd->grj", query_head, key_head, preferred_element_type=jnp.float32)
            * score_scale
        )
        scores = jnp.where(usable, scores, MASKED)
        maxima = jnp.max(scores, axis=2)
        weights = jnp.exp(scores - maxima[..., None])
        totals = jnp.sum(weights, axis=2)
        numerators = jnp.einsum(
            "grj,jd->grd",
            weights.astype(jnp.bfloat16),
            value_head,
            preferred_element_type=jnp.float32,
        )
        return (maxima, totals, numerators)

    maxima, totals, numerators = lax.map(one_head, (query_heads, key_heads, value_heads))
    summit, total_all, merged = combined_all((maxima, totals, numerators), "ctx", combine_pieces)
    attended = (
        (merged / total_all[..., None])
        .transpose(2, 0, 1, 3)
        .reshape(row_count, -1)
        .astype(jnp.bfloat16)
    )
    projected = lax.psum(jnp.dot(attended, w_out, preferred_element_type=jnp.float32), "tp")
    residual = stream + projected
    second_sum = lax.psum(jnp.sum(residual * residual, axis=1), "ctx")
    second_scale = lax.rsqrt(second_sum / D + EPSILON)[:, None]
    second_normed = (residual * ffn_gain).astype(jnp.bfloat16)
    gate_part = jnp.dot(second_normed, w_gate, preferred_element_type=jnp.float32)
    up_part = jnp.dot(second_normed, w_up, preferred_element_type=jnp.float32)
    gate_sum, up_sum = lax.psum((gate_part, up_part), "ctx")
    activated = (jax.nn.silu(second_scale * gate_sum) * (second_scale * up_sum)).astype(
        jnp.bfloat16
    )
    lowered = lax.psum(jnp.dot(activated, w_down, preferred_element_type=jnp.float32), "tp")
    result = residual + lowered
    present = jnp.arange(row_count)[:, None] < question_length[0]
    return jnp.where(present, result, 0.0).astype(jnp.bfloat16)


def solution(mesh):
    placed = (
        P(None, "ctx"),
        P("ctx"),
        P("ctx", "tp"),
        P("ctx", "tp"),
        P("ctx", "tp"),
        P("ctx"),
        P(),
        P("tp", "ctx"),
        P("ctx"),
        P("ctx", "tp"),
        P("ctx", "tp"),
        P("tp", "ctx"),
    )
    return jax.shard_map(
        body, mesh=mesh, in_specs=placed, out_specs=P(None, "ctx"), check_vma=False
    )
```

profile of v0, /device:TPU:1, one launch (start us, length us, event | category | flops | bytes accessed | tf_op | source)
XLA Modules:
  0.0 880.7 jit_solution(7069329605306751795)
XLA Ops:
  6.5 1.9 fusion.23
  10.0 122.7 %psum.49 = f32[64]{0:T(128)S(1)} all-reduce(f32[64]{0:T(128)S(1)} %fusion.21), channel_id=1, replica_groups=mesh['ctx'=64,'tp'=8] {'ctx'}, use_global_device_ids=true, to_apply=%region_1.0 | all-reduce | flops 64 | bytes 512 | tf_op jit(solution)/shard_map/psum | solution.py:55
  132.7 136.2 %all-reduce.4.cloned.1.call-done = f32[64,1024]{1,0:T(8,128)} async-done(((f32[64,1024]{1,0:T(8,128)}), f32[64,1024]{1,0:T(8,128)}) %all-reduce.4.cloned.1.call-update) | async-done | bytes 262160 | tf_op jit(solution)/shard_map/psum | solution.py:56
  270.0 1.3 fusion.27
  271.2 2.0 fusion.8
  273.3 64.7 %all-gather = f32[512,64]{1,0:T(8,128)S(1)} all-gather(f32[8,64]{1,0:T(8,128)S(1)} %get-tuple-element.251), channel_id=2, replica_groups=mesh['ctx'=64,'tp'=8] {'ctx'}, dimensions={0}, use_global_device_ids=true | all-gather | bytes 133120 | tf_op jit(solution)/shard_map/all_gather | solution.py:17
  338.3 71.3 %all-gather.1 = f32[512,64]{1,0:T(8,128)S(1)} all-gather(f32[8,64]{1,0:T(8,128)S(1)} %fusion.7), channel_id=3, replica_groups=mesh['ctx'=64,'tp'=8] {'ctx'}, dimensions={0}, use_global_device_ids=true | all-gather | bytes 133120 | tf_op jit(solution)/shard_map/all_gather | solution.py:17
  409.7 63.4 %all-gather.5.cloned.1.call-done = f32[512,64,128]{2,1,0:T(8,128)} async-done(((f32[8,64,128]{2,1,0:T(8,128)}), f32[512,64,128]{2,1,0:T(8,128)}) %all-gather.5.cloned.1.call-update) | async-done | bytes 16777232 | tf_op jit(solution)/shard_map/all_gather | solution.py:17
  474.0 81.3 %while.12 = (s32[]{:T(128)}, f32[1,8,64]{2,1,0:T(8,128)S(1)}, f32[1,8,64]{2,1,0:T(8,128)S(1)}, f32[1,8,64,128]{3,2,1,0:T(8,128)S(1)}, f32[64,1,8,64]{3,2,1,0:T(8...) while((s32[]{:T(128)}, f32[1,8,64]{2,1,0:T(8,128)S(1)}, ...), condition=%wide.region_6.7_spmd, body=%wide.region_5.6_spmd.sunk | while | flops 200197 | bytes 817307 | solution.py:22
  474.1 1.2 fusion.42
  475.4 1.2 fusion.42
  476.7 1.2 fusion.42
  478.0 1.2 fusion.42
  479.2 1.2 fusion.42
  480.5 1.2 fusion.42
  481.8 1.2 fusion.42
  483.1 1.2 fusion.42
  484.4 1.2 fusion.42
  485.7 1.2 fusion.42
  487.0 1.2 fusion.42
  488.3 1.2 fusion.42
  489.6 1.2 fusion.42
  490.9 1.2 fusion.42
  492.1 1.2 fusion.42
  493.4 1.2 fusion.42
  494.7 1.2 fusion.42
  496.0 1.2 fusion.42
  497.3 1.2 fusion.42
  498.6 1.2 fusion.42
  499.9 1.2 fusion.42
  501.2 1.2 fusion.42
  502.5 1.2 fusion.42
  503.8 1.2 fusion.42
  505.0 1.2 fusion.42
  506.3 1.2 fusion.42
  507.6 1.2 fusion.42
  508.9 1.2 fusion.42
  510.2 1.2 fusion.42
  511.5 1.2 fusion.42
  512.8 1.2 fusion.42
  514.1 1.2 fusion.42
  515.4 1.2 fusion.42
  516.7 1.2 fusion.42
  517.9 1.2 fusion.42
  519.2 1.2 fusion.42
  520.5 1.2 fusion.42
  521.8 1.2 fusion.42
  523.1 1.2 fusion.42
  524.4 1.2 fusion.42
  525.7 1.2 fusion.42
  527.0 1.2 fusion.42
  528.3 1.2 fusion.42
  529.6 1.2 fusion.42
  530.8 1.2 fusion.42
  532.1 1.2 fusion.42
  533.4 1.2 fusion.42
  534.7 1.2 fusion.42
  536.0 1.2 fusion.42
  556.7 22.6 %psum.51 = f32[64,128]{1,0:T(8,128)S(1)} all-reduce(f32[64,128]{1,0:T(8,128)S(1)} %fusion.13), channel_id=1, replica_groups=mesh['ctx'=64,'tp'=8] {'tp'}, use_global_device_ids=true, to_apply=%region_7.8 | all-reduce | flops 8192 | bytes 65536 | tf_op jit(solution)/shard_map/psum | solution.py:94
  581.1 2.0 fusion.28
  583.8 112.4 %psum.52 = f32[64]{0:T(128)S(1)} all-reduce(f32[64]{0:T(128)S(1)} %get-tuple-element.249), channel_id=1, replica_groups=mesh['ctx'=64,'tp'=8] {'ctx'}, use_global_device_ids=true, to_apply=%region_9.10 | all-reduce | flops 64 | bytes 512 | tf_op jit(solution)/shard_map/psum | solution.py:96
  696.2 144.7 %all-reduce.6.cloned.1.call-done = (f32[64,1792]{1,0:T(8,128)}, f32[64,1792]{1,0:T(8,128)}) async-done(((f32[64,1792]{1,0:T(8,128)}, f32[64,1792]{1,0:T(8,128)}), (f32[64,1792]{1,0:T(8,128)}, f32[64,1792]{1,0:T(8,128)})) %all-reduce.6.cloned.1.call-update) | async-done | bytes 917520 | tf_op jit(solution)/shard_map/psum | solution.py:101
  840.9 1.6 fusion.11
  842.5 30.9 %psum.55 = f32[64,128]{1,0:T(8,128)S(1)} all-reduce(f32[64,128]{1,0:T(8,128)S(1)} %fusion.11), channel_id=1, replica_groups=mesh['ctx'=64,'tp'=8] {'tp'}, use_global_device_ids=true, to_apply=%region_12.13 | all-reduce | flops 8192 | bytes 65536 | tf_op jit(solution)/shard_map/psum | solution.py:105
  (230 shorter events, 26.3 us)
Async XLA Ops:
  6.5 573.5 %copy-start = (bf16[128,1792]{1,0:T(8,128)(2,1)S(1)}, bf16[128,1792]{1,0:T(8,128)(2,1)}, u32[]{:S(2)}) copy-start(bf16[128,1792]{1,0:T(8,128)(2,1)} %param.24) | copy-start | bytes 1376260
  6.5 866.9 %copy-start.1 = (bf16[64,128]{1,0:T(8,128)(2,1)S(1)}, bf16[64,128]{1,0:T(8,128)(2,1)}, u32[]{:S(2)}) copy-start(bf16[64,128]{1,0:T(8,128)(2,1)} %param.14) | copy-start | bytes 49156
  6.5 262.3 %all-reduce.4.cloned.1.call-start = ((), (), s32[]{:S(2)}) async-start(), calls=%async_computation | async-start | bytes 524288 | tf_op jit(solution)/shard_map/psum | solution.py:56
  8.5 464.6 %all-gather.5.cloned.1.call-start = ((), (), s32[]{:S(2)}) async-start(), calls=%async_computation.1 | async-start | bytes 17039360 | tf_op jit(solution)/shard_map/all_gather | solution.py:17
  273.2 567.7 %all-reduce.6.cloned.1.call-start = ((), (), s32[]{:S(2)}) async-start(), calls=%async_computation.2 | async-start | bytes 1835008 | tf_op jit(solution)/shard_map/psum | solution.py:101
Sparse Core Ops, SparseCore 0:
  10.8 258.0 all-reduce.3
  273.3 199.6 all-gather.4
  583.3 257.6 all-reduce.5
where the time goes:
time: 884 us; the launch traced here: 881 us
  blocking collectives  425 us (48%)
  waiting for transfers between devices  344 us (39%)
  other arithmetic  82.2 us (9%)
  between operations  14.5 us (2%)
  matrix products  10.9 us (1%)
    psum x1, waiting for transfers between devices, body(): gate_sum, up_sum = lax.psum((gate_part, up_part), 'ctx')  145 us
    psum x1, waiting for transfers between devices, body(): query_sum = lax.psum(query_part, 'ctx')  136 us
    all_gather x2, blocking collectives, combined_all(): gathered = jax.tree.map(lambda a: lax.all_gather(a, axis), part)  136 us
    psum x1, blocking collectives, body(): square_sum = lax.psum(square_part, 'ctx')  123 us
    psum x1, blocking collectives, body(): second_sum = lax.psum(jnp.sum(residual * residual, axis=1), 'ctx')  112 us
    add x63, other arithmetic, combine_pieces(): first[2] * first_factor[..., None] + second[2] * second_factor[..., None]  76.4 us
    all_gather x1, waiting for transfers between devices, combined_all(): gathered = jax.tree.map(lambda a: lax.all_gather(a, axis), part)  63.4 us
    psum x1, blocking collectives, body(): lax.psum(jnp.dot(activated, w_down, preferred_element_type=jnp.float32),...  30.9 us
  transfers between devices with their start and end apart: 3, of which 3 were waited for; matrix products, arithmetic and copies ran while one was open for 0% of the time, Pallas kernels for 0%

commit v1 on v0

v1 whole, which is shorter than its diff:
```python
import math

import jax
import jax.numpy as jnp
from jax import lax
from jax.experimental import pallas as pl
from jax.experimental.pallas import tpu as pltpu
from jax.sharding import PartitionSpec as P

D = 8192
HD = 128
EPSILON = 1e-05
MASKED = -1e30
NX = 4
NZ = 16
NT = 8
ROWS = 64
HEAD_CHUNKS = 8
FF_BLOCKS = 14
MESH = pl.DeviceIdType.MESH
F32 = jnp.float32
BF16 = jnp.bfloat16


def lane_row(column):
    shape = (column.shape[0], 128)
    same = lax.broadcasted_iota(jnp.int32, shape, 0) == lax.broadcasted_iota(jnp.int32, shape, 1)
    return jnp.sum(jnp.where(same, jnp.broadcast_to(column, shape), 0.0), axis=0, keepdims=True)


def row_column(row, base):
    shape = (16, 128)
    same = lax.broadcasted_iota(jnp.int32, shape, 0) + base == lax.broadcasted_iota(
        jnp.int32, shape, 1
    )
    return jnp.sum(jnp.where(same, jnp.broadcast_to(row, shape), 0.0), axis=1, keepdims=True)


def kernel(
    length_ref,
    hidden_ref,
    attn_gain_ref,
    ffn_gain_ref,
    wq_hbm,
    key_hbm,
    value_hbm,
    wout_hbm,
    wgate_hbm,
    wup_hbm,
    wdown_hbm,
    out_ref,
    wq,
    key,
    value,
    wout,
    wgate,
    wup,
    wdown,
    load_sems,
    send_sems,
    qx_src,
    qx_dst,
    qz_src,
    qz_dst,
    q_all,
    sx_src,
    sx_dst,
    sz_src,
    sz_dst,
    ax_src,
    ax_dst,
    az_src,
    az_dst,
    a_all,
    tx_src,
    tx_dst,
    tz_src,
    tz_dst,
    p_all,
    fx_src,
    fx_dst,
    fz_src,
    fz_dst,
    f_all,
    ux_src,
    ux_dst,
    uz_src,
    uz_dst,
    d_all,
    recv_sems,
    q_gather_sems,
    a_gather_sems,
    f_gather_sems,
    x_gather_sems,
    p_sems,
    d_sems,
):
    ctx = lax.axis_index("ctx")
    tp = lax.axis_index("tp")
    x = lax.rem(ctx, NX)
    z = lax.div(ctx, NX)

    def x_peer(k):
        return z * NX + lax.rem(x + k, NX)

    def z_peer(k):
        return lax.rem(z + k, NZ) * NX + x

    def t_peer(k):
        return lax.rem(tp + k, NT)

    loads = [
        pltpu.make_async_copy(source, target, load_sems.at[at])
        for at, (source, target) in enumerate(
            [
                (wq_hbm, wq),
                (key_hbm, key),
                (value_hbm, value),
                (wout_hbm, wout),
                (wgate_hbm, wgate),
                (wup_hbm, wup),
                (wdown_hbm, wdown),
            ]
        )
    ]
    for load in loads:
        load.start()

    barrier = pltpu.get_barrier_semaphore()
    for k in range(1, NX):
        pl.semaphore_signal(barrier, inc=1, device_id=(x_peer(k), tp), device_id_type=MESH)
    for k in range(1, NT):
        pl.semaphore_signal(barrier, inc=1, device_id=(ctx, t_peer(k)), device_id_type=MESH)

    def greet(k, carry):
        pl.semaphore_signal(barrier, inc=1, device_id=(z_peer(k), tp), device_id_type=MESH)
        return carry

    lax.fori_loop(1, NZ, greet, 0)

    def send(source, target, send_sem, recv_sem, device):
        pltpu.make_async_remote_copy(
            src_ref=source,
            dst_ref=target,
            send_sem=send_sem,
            recv_sem=recv_sem,
            device_id=device,
            device_id_type=MESH,
        ).start()

    def drain(ref, sem):
        pltpu.make_async_copy(ref, ref, sem).wait()

    stream = hidden_ref[...].astype(F32)
    sx_src[...] = lane_row(jnp.sum(stream * stream, axis=1, keepdims=True))
    normed = (stream * attn_gain_ref[...]).astype(BF16)
    loads[0].wait()
    query_part = jnp.dot(normed, wq[...], preferred_element_type=F32)
    for j in range(NX):
        for h in range(2):
            for g in range(4):
                column = (2 * j + h) * HD
                qx_src[j, 4 * h + g] = query_part[16 * g : 16 * g + 16, column : column + HD]
    pl.semaphore_wait(barrier, NX - 1 + NZ - 1 + NT - 1)

    def x_scatter(source, target, at):
        for k in range(1, NX):
            send(
                source.at[lax.rem(x + k, NX)],
                target.at[k - 1],
                send_sems.at[at],
                recv_sems.at[at],
                (x_peer(k), tp),
            )

    def x_same(source, target, at):
        for k in range(1, NX):
            send(source, target.at[k - 1], send_sems.at[at], recv_sems.at[at], (x_peer(k), tp))

    def reducer_step(count, stride):
        start = lax.div(z + stride - 1, stride)

        def visit(step, body):
            chunk = lax.rem(start + step, count)
            target = chunk * stride
            offset = lax.rem(target - z + NZ, NZ)

            @pl.when(offset != 0)
            def _():
                body(chunk, offset - 1, (target * NX + x, tp))

        return visit

    def z_scatter(source, target, at, row_source, row_target, row_at, count, stride):
        visit = reducer_step(count, stride)

        def step(s, carry):
            def body(chunk, slot, device):
                send(row_source, row_target.at[slot], send_sems.at[row_at], recv_sems.at[row_at], device)
                send(source.at[chunk], target.at[slot], send_sems.at[at], recv_sems.at[at], device)

            visit(s, body)
            return carry

        lax.fori_loop(0, count, step, 0)

    def z_gather(whole, chunk, at, sems):
        def step(k, carry):
            send(
                whole.at[x, chunk],
                whole.at[x, chunk],
                send_sems.at[at],
                sems.at[chunk],
                (z_peer(k), tp),
            )
            return carry

        lax.fori_loop(1, NZ, step, 0)

    def z_gather_wait(whole, sems, count, stride):
        def step(chunk, carry):
            @pl.when(chunk * stride != z)
            def _():
                drain(whole.at[x, chunk], sems.at[chunk])

            return carry

        lax.fori_loop(0, count, step, 0)

    def x_gather(whole, at, sem_at):
        for k in range(1, NX):
            send(
                whole.at[x],
                whole.at[x],
                send_sems.at[at],
                x_gather_sems.at[sem_at + k - 1],
                (x_peer(k), tp),
            )
        for k in range(1, NX):
            drain(whole.at[lax.rem(x + NX - k, NX)], x_gather_sems.at[sem_at + k - 1])

    x_same(sx_src, sx_dst, 0)
    x_scatter(qx_src, qx_dst, 1)
    drain(sx_dst, recv_sems.at[0])
    sz_src[...] = sx_src[...] + sx_dst[0] + sx_dst[1] + sx_dst[2]
    drain(qx_dst, recv_sems.at[1])
    qz_src[...] = qx_src[x] + qx_dst[0] + qx_dst[1] + qx_dst[2]
    z_scatter(qz_src, qz_dst, 3, sz_src, sz_dst, 2, HEAD_CHUNKS, 2)
    even = lax.rem(z, 2) == 0
    half = lax.div(z, 2)

    @pl.when(even)
    def _():
        drain(sz_dst, recv_sems.at[2])
        squares = jnp.sum(sz_dst[...], axis=0) + sz_src[...]
        scale = lax.rsqrt(row_column(squares, 16 * lax.rem(half, 4)) / D + EPSILON)
        drain(qz_dst, recv_sems.at[3])
        total = qz_src[half] + jnp.sum(qz_dst[...], axis=0)
        q_all[x, half] = (scale * total).astype(BF16)
        z_gather(q_all, half, 4, q_gather_sems)

    z_gather_wait(q_all, q_gather_sems, HEAD_CHUNKS, 2)
    x_gather(q_all, 5, 0)

    loads[1].wait()
    loads[2].wait()
    queries = q_all[...].reshape(NX * HEAD_CHUNKS * 16, HD)
    scores = lax.dot_general(
        key[...], queries, (((1,), (1,)), ((), ())), preferred_element_type=F32
    ) * (1.0 / math.sqrt(HD))
    usable = lax.broadcasted_iota(jnp.int32, scores.shape, 0) < length_ref[0]
    scores = jnp.where(usable, scores, MASKED)
    maxima = jnp.max(scores, axis=0, keepdims=True)
    weights = jnp.exp(scores - maxima)
    totals = jnp.sum(weights, axis=0, keepdims=True)
    for j in range(NX):
        tx_src[j, 0] = maxima[:, 128 * j : 128 * j + 128]
        tx_src[j, 1] = totals[:, 128 * j : 128 * j + 128]
    x_scatter(tx_src, tx_dst, 6)
    numerators = lax.dot_general(
        value[...], weights.astype(BF16), (((0,), (0,)), ((), ())), preferred_element_type=F32
    ).astype(BF16)
    for j in range(NX):
        for i in range(HEAD_CHUNKS):
            ax_src[j, i] = numerators[16 * i : 16 * i + 16, 128 * j : 128 * j + 128]
    x_scatter(ax_src, ax_dst, 7)
    drain(tx_dst, recv_sems.at[6])
    pieces = [tx_src.at[x]] + [tx_dst.at[k] for k in range(NX - 1)]
    summit = pieces[0][0]
    for piece in pieces[1:]:
        summit = jnp.maximum(summit, piece[0])
    factors = [jnp.exp(piece[0] - summit) for piece in pieces]
    tz_src[0] = summit
    tz_src[1] = sum(factor * piece[1] for factor, piece in zip(factors, pieces))
    drain(ax_dst, recv_sems.at[7])
    merged = ax_src[x].astype(F32) * factors[0]
    for k in range(NX - 1):
        merged = merged + ax_dst[k].astype(F32) * factors[k + 1]
    az_src[...] = merged.astype(BF16)
    z_scatter(az_src, az_dst, 9, tz_src, tz_dst, 8, HEAD_CHUNKS, 2)

    @pl.when(even)
    def _():
        drain(tz_dst, recv_sems.at[8])
        own = tz_src[0]
        others = tz_dst[:, 0]
        summit = jnp.maximum(own, jnp.max(others, axis=0))
        own_factor = jnp.exp(own - summit)
        factors = jnp.exp(others - summit)
        total = own_factor * tz_src[1] + jnp.sum(factors * tz_dst[:, 1], axis=0)
        drain(az_dst, recv_sems.at[9])
        merged = own_factor * az_src[half].astype(F32) + jnp.sum(
            factors * az_dst[...].astype(F32), axis=0
        )
        a_all[x, half] = (merged / total).astype(BF16)
        z_gather(a_all, half, 10, a_gather_sems)

    z_gather_wait(a_all, a_gather_sems, HEAD_CHUNKS, 2)
    x_gather(a_all, 11, 3)

    loads[3].wait()
    projected = jnp.zeros((ROWS, HD), F32)
    for j in range(NX):
        turned = jnp.transpose(a_all[j].reshape(HD, 128).astype(F32)).astype(BF16)
        for h in range(2):
            at = (2 * j + h) * HD
            projected = projected + jnp.dot(
                turned[ROWS * h : ROWS * h + ROWS],
                wout[at : at + HD],
                preferred_element_type=F32,
            )

    def tp_sum(part, whole, at, sems):
        whole[tp] = part.astype(BF16)
        for k in range(1, NT):
            send(whole.at[tp], whole.at[tp], send_sems.at[at], sems.at[tp], (ctx, t_peer(k)))
        for k in range(1, NT):
            source = t_peer(k)
            drain(whole.at[source], sems.at[source])
        total = whole[0].astype(F32)
        for source in range(1, NT):
            total = total + whole[source].astype(F32)
        return total

    residual = hidden_ref[...].astype(F32) + tp_sum(projected, p_all, 12, p_sems)

    ux_src[...] = lane_row(jnp.sum(residual * residual, axis=1, keepdims=True))
    x_same(ux_src, ux_dst, 13)
    second = (residual * ffn_gain_ref[...]).astype(BF16)
    loads[4].wait()
    loads[5].wait()
    for kind, weight in enumerate((wgate, wup)):
        part = jnp.dot(second, weight[...], preferred_element_type=F32).astype(BF16)
        for j in range(NX):
            for b in range(FF_BLOCKS):
                fx_src[j, b, kind] = part[16 * j : 16 * j + 16, 128 * b : 128 * b + 128]
    x_scatter(fx_src, fx_dst, 14)
    drain(ux_dst, recv_sems.at[13])
    uz_src[...] = ux_src[...] + ux_dst[0] + ux_dst[1] + ux_dst[2]
    drain(fx_dst, recv_sems.at[14])
    fz_src[...] = (
        fx_src[x].astype(F32)
        + fx_dst[0].astype(F32)
        + fx_dst[1].astype(F32)
        + fx_dst[2].astype(F32)
    ).astype(BF16)
    z_scatter(fz_src, fz_dst, 16, uz_src, uz_dst, 15, FF_BLOCKS, 1)

    @pl.when(z < FF_BLOCKS)
    def _():
        drain(uz_dst, recv_sems.at[15])
        squares = jnp.sum(uz_dst[...], axis=0) + uz_src[...]
        scale = lax.rsqrt(row_column(squares, 16 * x) / D + EPSILON)
        drain(fz_dst, recv_sems.at[16])
        both = fz_src[z].astype(F32) + jnp.sum(fz_dst[...].astype(F32), axis=0)
        gate = scale * both[0]
        up = scale * both[1]
        f_all[x, z] = (gate / (1.0 + jnp.exp(-gate)) * up).astype(BF16)
        z_gather(f_all, z, 17, f_gather_sems)

    z_gather_wait(f_all, f_gather_sems, FF_BLOCKS, 1)
    x_gather(f_all, 18, 6)

    loads[6].wait()
    lowered = jnp.zeros((ROWS, HD), F32)
    for b in range(FF_BLOCKS):
        lowered = lowered + jnp.dot(
            f_all[:, b].reshape(ROWS, 128),
            wdown[128 * b : 128 * b + 128],
            preferred_element_type=F32,
        )
    result = residual + tp_sum(lowered, d_all, 19, d_sems)
    out_ref[...] = result.astype(BF16)

    for at, ref in (
        (0, sx_dst),
        (1, qx_dst),
        (5, q_all.at[pl.ds(0, 3)]),
        (6, tx_dst),
        (7, ax_dst),
        (11, a_all.at[pl.ds(0, 3)]),
        (12, p_all.at[pl.ds(0, 7)]),
        (13, ux_dst),
        (14, fx_dst),
        (18, f_all.at[pl.ds(0, 3)]),
        (19, d_all.at[pl.ds(0, 7)]),
    ):
        drain(ref, send_sems.at[at])

    @pl.when(even)
    def _():
        for at, ref in (
            (2, sz_dst),
            (3, qz_dst),
            (8, tz_dst),
            (9, az_dst),
        ):
            drain(ref.at[pl.ds(0, HEAD_CHUNKS - 1)], send_sems.at[at])
        drain(az_dst, send_sems.at[4])
        drain(az_dst, send_sems.at[10])

    @pl.when(jnp.logical_not(even))
    def _():
        for at, ref in (
            (2, sz_dst),
            (3, qz_dst),
            (8, tz_dst),
            (9, az_dst),
        ):
            drain(ref.at[pl.ds(0, HEAD_CHUNKS)], send_sems.at[at])

    @pl.when(z < FF_BLOCKS)
    def _():
        drain(uz_dst.at[pl.ds(0, FF_BLOCKS - 1)], send_sems.at[15])
        drain(fz_dst.at[pl.ds(0, FF_BLOCKS - 1)], send_sems.at[16])
        drain(az_dst, send_sems.at[17])

    @pl.when(z >= FF_BLOCKS)
    def _():
        drain(uz_dst.at[pl.ds(0, FF_BLOCKS)], send_sems.at[15])
        drain(fz_dst.at[pl.ds(0, FF_BLOCKS)], send_sems.at[16])


def body(
    hidden_in,
    attn_gain,
    w_query,
    key_cache,
    value_cache,
    block_lengths,
    question_length,
    w_out,
    ffn_gain,
    w_gate,
    w_up,
    w_down,
):
    vmem = pl.BlockSpec(memory_space=pltpu.VMEM)
    anywhere = pl.BlockSpec(memory_space=pl.ANY)
    weights = (w_query, key_cache, value_cache, w_out, w_gate, w_up, w_down)
    chunk = (16, 128)
    row = (1, 128)
    scratch = [pltpu.VMEM(a.shape, a.dtype) for a in weights]
    scratch += [pltpu.SemaphoreType.DMA((7,)), pltpu.SemaphoreType.DMA((20,))]
    scratch += [
        pltpu.VMEM((NX, HEAD_CHUNKS) + chunk, F32),
        pltpu.VMEM((NX - 1, HEAD_CHUNKS) + chunk, F32),
        pltpu.VMEM((HEAD_CHUNKS,) + chunk, F32),
        pltpu.VMEM((NZ - 1,) + chunk, F32),
        pltpu.VMEM((NX, HEAD_CHUNKS) + chunk, BF16),
        pltpu.VMEM(row, F32),
        pltpu.VMEM((NX - 1,) + row, F32),
        pltpu.VMEM(row, F32),
        pltpu.VMEM((NZ - 1,) + row, F32),
        pltpu.VMEM((NX, HEAD_CHUNKS) + chunk, BF16),
        pltpu.VMEM((NX - 1, HEAD_CHUNKS) + chunk, BF16),
        pltpu.VMEM((HEAD_CHUNKS,) + chunk, BF16),
        pltpu.VMEM((NZ - 1,) + chunk, BF16),
        pltpu.VMEM((NX, HEAD_CHUNKS) + chunk, BF16),
        pltpu.VMEM((NX, 2) + row, F32),
        pltpu.VMEM((NX - 1, 2) + row, F32),
        pltpu.VMEM((2,) + row, F32),
        pltpu.VMEM((NZ - 1, 2) + row, F32),
        pltpu.VMEM((NT, ROWS, 128), BF16),
        pltpu.VMEM((NX, FF_BLOCKS, 2) + chunk, BF16),
        pltpu.VMEM((NX - 1, FF_BLOCKS, 2) + chunk, BF16),
        pltpu.VMEM((FF_BLOCKS, 2) + chunk, BF16),
        pltpu.VMEM((NZ - 1, 2) + chunk, BF16),
        pltpu.VMEM((NX, FF_BLOCKS) + chunk, BF16),
        pltpu.VMEM(row, F32),
        pltpu.VMEM((NX - 1,) + row, F32),
        pltpu.VMEM(row, F32),
        pltpu.VMEM((NZ - 1,) + row, F32),
        pltpu.VMEM((NT, ROWS, 128), BF16),
        pltpu.SemaphoreType.DMA((17,)),
        pltpu.SemaphoreType.DMA((HEAD_CHUNKS,)),
        pltpu.SemaphoreType.DMA((HEAD_CHUNKS,)),
        pltpu.SemaphoreType.DMA((FF_BLOCKS,)),
        pltpu.SemaphoreType.DMA((9,)),
        pltpu.SemaphoreType.DMA((NT,)),
        pltpu.SemaphoreType.DMA((NT,)),
    ]
    result = pl.pallas_call(
        kernel,
        out_shape=jax.ShapeDtypeStruct(hidden_in.shape, BF16),
        in_specs=[pl.BlockSpec(memory_space=pltpu.SMEM)] + [vmem] * 3 + [anywhere] * 7,
        out_specs=vmem,
        scratch_shapes=scratch,
        compiler_params=pltpu.CompilerParams(
            collective_id=0, has_side_effects=True, vmem_limit_bytes=32 * 1024 * 1024
        ),
    )(
        block_lengths,
        hidden_in,
        attn_gain.reshape(1, -1),
        ffn_gain.reshape(1, -1),
        *weights,
    )
    present = jnp.arange(ROWS)[:, None] < question_length[0]
    return jnp.where(present, result, jnp.zeros_like(result))


def solution(mesh):
    placed = (
        P(None, "ctx"),
        P("ctx"),
        P("ctx", "tp"),
        P("ctx", "tp"),
        P("ctx", "tp"),
        P("ctx"),
        P(),
        P("tp", "ctx"),
        P("ctx"),
        P("ctx", "tp"),
        P("ctx", "tp"),
        P("tp", "ctx"),
    )
    return jax.shard_map(
        body, mesh=mesh, in_specs=placed, out_specs=P(None, "ctx"), check_vma=False
    )
```

time: 884 us -> 118 us (0.13)
  blocking collectives: 425 us -> 0 us
  waiting for transfers between devices: 344 us -> 0 us
  Pallas kernels: 0 us -> 107 us
  other arithmetic: 82.2 us -> 0.69 us
  between operations: 14.5 us -> 1.34 us
  matrix products: 10.9 us -> 0 us
    psum x4 -> x0, blocking collectives: 289 us -> none  [the longest x1 123 us: body(): square_sum = lax.psum(square_part, 'ctx')]
    psum x2 -> x0, waiting for transfers between devices: 281 us -> none  [the longest x1 145 us: body(): gate_sum, up_sum = lax.psum((gate_part, up_part), 'ctx')]
    all_gather x2 -> x0, blocking collectives: 136 us -> none  [combined_all(): gathered = jax.tree.map(lambda a: lax.all_gather(a, axis), part)]
    pallas_call x0 -> x1, Pallas kernels: none -> 107 us  [body(): pl.pallas_call(kernel, out_shape=jax.ShapeDtypeStruct(hidden_in.shape, BF...]
    add x63 -> x0, other arithmetic: 76.4 us -> none  [combine_pieces(): first[2] * first_factor[..., None] + second[2] * second_factor[..., None]]
    all_gather x1 -> x0, waiting for transfers between devices: 63.4 us -> none  [combined_all(): gathered = jax.tree.map(lambda a: lax.all_gather(a, axis), part)]
    dot_general x7 -> x0, matrix products: 10.9 us -> none  [the longest x1 2.03 us: body(): jnp.dot(second_normed, w_gate, preferred_element_type=jnp.float32)]
  transfers between devices with their start and end apart: 3 -> 0, of which waited for: 3 -> 0; matrix products, arithmetic and copies ran while one was open for 0% -> 0% of each run, Pallas kernels for 0% -> 0%
where the time goes in v1:
time: 118 us; the launch traced here: 117 us
  Pallas kernels  107 us (91%)
  local copies, waits for them, and re-layouts  8.13 us (7%)
  between operations  1.34 us (1%)
    pallas_call x1, Pallas kernels, body(): pl.pallas_call(kernel, out_shape=jax.ShapeDtypeStruct(hidden_in.shape, BF...  107 us
    unnamed x20, local copies, waits for them, and re-layouts  8.13 us

profile of v1, /device:TPU:1, one launch (start us, length us, event | category | flops | bytes accessed | tf_op | source)
XLA Modules:
  0.0 117.2 jit_solution(17549477770183365661)
XLA Ops:
  1.3 0.0 copy-start.8
  1.3 0.0 copy-start.9
  1.3 0.6 copy-done.8
  2.0 0.0 copy-done.9
  2.0 0.0 copy-start
  2.0 1.0 copy-done
  3.0 0.0 copy-start.1
  3.0 1.0 copy-done.1
  4.0 0.0 copy-start.2
  4.0 1.0 copy-done.2
  5.0 0.0 copy-start.3
  5.0 0.9 copy-done.3
  6.0 0.0 copy-start.4
  6.0 0.9 copy-done.4
  6.9 0.0 copy-start.5
  6.9 0.9 copy-done.5
  7.8 0.0 copy-start.6
  7.8 0.9 copy-done.6
  8.8 0.0 copy-start.7
  8.8 0.7 copy-done.7
  9.5 107.1 %shard_map.118 = bf16[64,128]{1,0:T(8,128)(2,1)S(1)} custom-call(s32[1]{0:T(128)S(6)} %copy.13.length_ref, bf16[64,128]{1,0:T(8,128)(2,1)S(1)} %copy-done.7, f32[1,128]{1,0:T(1,128)S(1)} %bitcast.4, f32[1,128]{1,0:T(1,128)S(1)} %bitcast.5, bf16[128,1024]{1,0:T(8,128)(2,1)S(1)} %copy-done.3, bf16[512,128]{1,0:T(8,128)(2,1)S(1)} %copy-done.5, ...), custom_call_target="tpu_custom_call" | custom-call | tf_op jit(solution)/shard_map/pallas_call | solution.py:503
  116.6 0.7 broadcast_select_fusion
  (1 shorter events, 0.0 us)
Async XLA Ops:
  1.3 0.7 copy-start.8
  1.3 0.7 copy-start.9
  2.0 1.0 copy-start
  3.0 1.0 copy-start.1
  4.0 1.0 copy-start.2
  5.0 0.9 copy-start.3
  6.0 0.9 copy-start.4
  6.9 0.9 copy-start.5
  7.8 0.9 copy-start.6
  8.8 0.7 copy-start.7

commit v2 on v0

v2 whole, which is shorter than its diff:
```python
import functools
import math

import jax
import jax.numpy as jnp
from jax import lax
from jax.experimental import pallas as pl
from jax.experimental.pallas import tpu as pltpu
from jax.sharding import PartitionSpec as P

D = 8192
HD = 128
EPSILON = 1e-05
MASKED = -1e30
NX = 4
NZ = 16
NT = 8
ROWS = 64
CHUNKS = 8
FF_BLOCKS = 14
PIECES = 4
PIECE = NZ // PIECES
FAR_FIRST = (8, 7, 9, 6, 10, 5, 11, 4, 12, 3, 13, 2, 14, 1, 15)
NEAR = tuple(
    (dz % NZ, dx)
    for dz in (4, 3, -3, 2, -2, 1, -1, 0)
    for dx in (2, 1, 3, 0)
    if (dz, dx) != (0, 0)
)
NEAR_ONE_WAY = tuple((dz, dx) for dz, dx in NEAR if dz == 4 and dx != 0)
PARTNERS = NX - 1 + NZ - 1 + NT - 1 + 7 * 3 + 3
MESH = pl.DeviceIdType.MESH
F32 = jnp.float32
BF16 = jnp.bfloat16


def lane_row(column):
    shape = (column.shape[0], 128)
    same = lax.broadcasted_iota(jnp.int32, shape, 0) == lax.broadcasted_iota(jnp.int32, shape, 1)
    return jnp.sum(jnp.where(same, jnp.broadcast_to(column, shape), 0.0), axis=0, keepdims=True)


def row_column(row, base):
    shape = (16, 128)
    same = lax.broadcasted_iota(jnp.int32, shape, 0) + base == lax.broadcasted_iota(
        jnp.int32, shape, 1
    )
    return jnp.sum(jnp.where(same, jnp.broadcast_to(row, shape), 0.0), axis=1, keepdims=True)


def kernel(
    length_ref,
    hidden_hbm,
    attn_gain_hbm,
    ffn_gain_hbm,
    wq_hbm,
    key_hbm,
    value_hbm,
    wout_hbm,
    wgate_hbm,
    wup_hbm,
    wdown_hbm,
    out_ref,
    hidden,
    attn_gain,
    ffn_gain,
    wq,
    key,
    value,
    wout,
    wgate,
    wup,
    wdown,
    load_sems,
    send_sems,
    recv_sems,
    qx_src,
    qx_dst,
    qz_src,
    qz_dst,
    q_all,
    sx_src,
    sx_dst,
    sz_src,
    sz_dst,
    ax_src,
    ax_dst,
    az_src,
    az_dst,
    a_all,
    tx_src,
    tx_dst,
    tz_src,
    tz_dst,
    p_all,
    fx_src,
    fx_dst,
    fz_src,
    fz_dst,
    f_all,
    ux_src,
    ux_dst,
    uz_src,
    uz_dst,
    d_all,
    f_gather_sems,
    p_sems,
    d_sems,
):
    ctx = lax.axis_index("ctx")
    tp = lax.axis_index("tp")
    x = lax.rem(ctx, NX)
    z = lax.div(ctx, NX)

    def x_of(k):
        return lax.rem(x + k, NX)

    def z_of(k):
        return lax.rem(z + k, NZ)

    def t_of(k):
        return lax.rem(tp + k, NT)

    def device(dz, dx):
        return (z_of(dz) * NX + x_of(dx), tp)

    sources = (
        hidden_hbm,
        attn_gain_hbm,
        wq_hbm,
        key_hbm,
        value_hbm,
        ffn_gain_hbm,
        wout_hbm,
        wgate_hbm,
        wup_hbm,
        wdown_hbm,
    )
    targets = (hidden, attn_gain, wq, key, value, ffn_gain, wout, wgate, wup, wdown)
    loads = [
        pltpu.make_async_copy(source, target, load_sems.at[at])
        for at, (source, target) in enumerate(zip(sources, targets))
    ]
    for load in loads[:3]:
        load.start()

    barrier = pltpu.get_barrier_semaphore()

    def greet(peer):
        pl.semaphore_signal(barrier, inc=1, device_id=peer, device_id_type=MESH)

    for k in FAR_FIRST:
        greet(device(k, 0))
    for k in range(1, NX):
        greet(device(0, k))
    for k in range(1, NT):
        greet((ctx, t_of(k)))
    for dz, dx in NEAR:
        if dz != 0 and dx != 0:
            greet(device(dz, dx))
    for dz, dx in NEAR_ONE_WAY:
        greet(device(-dz % NZ, -dx % NX))
    for load in loads[3:]:
        load.start()

    def send(source, target, send_sem, recv_sem, peer):
        pltpu.make_async_remote_copy(
            src_ref=source,
            dst_ref=target,
            send_sem=send_sem,
            recv_sem=recv_sem,
            device_id=peer,
            device_id_type=MESH,
        ).start()

    def drain(ref, sem):
        pltpu.make_async_copy(ref, ref, sem).wait()

    pending = []

    def at_end(sem_at, ref, condition=None):
        pending.append((sem_at, ref, condition))

    def finish():
        for sem_at, ref, condition in pending:
            if condition is None:
                drain(ref, send_sems.at[sem_at])
            else:
                pl.when(condition)(functools.partial(drain, ref, send_sems.at[sem_at]))

    def x_scatter(source, target, at):
        for k in range(1, NX):
            send(source.at[x_of(k)], target.at[k - 1], send_sems.at[at], recv_sems.at[at], device(0, k))
        at_end(at, target)

    def x_same(source, target, at):
        for k in range(1, NX):
            send(source, target.at[k - 1], send_sems.at[at], recv_sems.at[at], device(0, k))
        at_end(at, target)

    def z_scatter(source, target, at, row_source, row_target, row_at):
        for k in FAR_FIRST:
            send(
                row_source,
                row_target.at[k - 1],
                send_sems.at[row_at],
                recv_sems.at[row_at],
                device(k, 0),
            )
            send(
                source.at[lax.rem(z + k, CHUNKS)],
                target.at[k - 1],
                send_sems.at[at],
                recv_sems.at[at],
                device(k, 0),
            )
        at_end(row_at, row_target)
        at_end(at, target)

    def near_gather(whole, at):
        own = x * CHUNKS + lax.rem(z, CHUNKS)
        for dz, dx in NEAR:
            send(whole.at[own], whole.at[own], send_sems.at[at], recv_sems.at[at], device(dz, dx))
        rest = whole.at[pl.ds(0, NX * CHUNKS - 1)]
        drain(rest, recv_sems.at[at])
        at_end(at, rest)

    loads[0].wait()
    loads[1].wait()
    stream = hidden[...].astype(F32)
    sx_src[...] = lane_row(jnp.sum(stream * stream, axis=1, keepdims=True))
    normed = (stream * attn_gain[...]).astype(BF16)
    loads[2].wait()
    query_part = jnp.dot(normed, wq[...], preferred_element_type=F32)
    for j in range(NX):
        for h in range(2):
            for g in range(4):
                column = (2 * j + h) * HD
                qx_src[j, 4 * h + g] = query_part[16 * g : 16 * g + 16, column : column + HD]
    pl.semaphore_wait(barrier, PARTNERS)

    x_same(sx_src, sx_dst, 0)
    x_scatter(qx_src, qx_dst, 1)
    drain(sx_dst, recv_sems.at[0])
    sz_src[...] = sx_src[...] + sx_dst[0] + sx_dst[1] + sx_dst[2]
    drain(qx_dst, recv_sems.at[1])
    qz_src[...] = qx_src[x] + qx_dst[0] + qx_dst[1] + qx_dst[2]
    z_scatter(qz_src, qz_dst, 3, sz_src, sz_dst, 2)
    mine = lax.rem(z, CHUNKS)
    slot = x * CHUNKS + mine
    drain(sz_dst, recv_sems.at[2])
    squares = jnp.sum(sz_dst[...], axis=0) + sz_src[...]
    scale = lax.rsqrt(row_column(squares, 16 * lax.rem(mine, 4)) / D + EPSILON)
    drain(qz_dst, recv_sems.at[3])
    total = qz_src[mine] + jnp.sum(qz_dst[...], axis=0)
    q_all[slot] = (scale * total).astype(BF16)
    near_gather(q_all, 4)

    loads[3].wait()
    loads[4].wait()
    queries = q_all[...].reshape(NX * CHUNKS * 16, HD)
    scores = lax.dot_general(
        key[...], queries, (((1,), (1,)), ((), ())), preferred_element_type=F32
    ) * (1.0 / math.sqrt(HD))
    usable = lax.broadcasted_iota(jnp.int32, scores.shape, 0) < length_ref[0]
    scores = jnp.where(usable, scores, MASKED)
    maxima = jnp.max(scores, axis=0, keepdims=True)
    weights = jnp.exp(scores - maxima)
    totals = jnp.sum(weights, axis=0, keepdims=True)
    for j in range(NX):
        tx_src[j, 0] = maxima[:, 128 * j : 128 * j + 128]
        tx_src[j, 1] = totals[:, 128 * j : 128 * j + 128]
    x_scatter(tx_src, tx_dst, 5)
    numerators = lax.dot_general(
        value[...], weights.astype(BF16), (((0,), (0,)), ((), ())), preferred_element_type=F32
    ).astype(BF16)
    for j in range(NX):
        for i in range(CHUNKS):
            ax_src[j, i] = numerators[16 * i : 16 * i + 16, 128 * j : 128 * j + 128]
    x_scatter(ax_src, ax_dst, 6)
    drain(tx_dst, recv_sems.at[5])
    pieces = [tx_src.at[x]] + [tx_dst.at[k] for k in range(NX - 1)]
    summit = pieces[0][0]
    for piece in pieces[1:]:
        summit = jnp.maximum(summit, piece[0])
    factors = [jnp.exp(piece[0] - summit) for piece in pieces]
    tz_src[0] = summit
    tz_src[1] = sum(factor * piece[1] for factor, piece in zip(factors, pieces))
    drain(ax_dst, recv_sems.at[6])
    merged = ax_src[x].astype(F32) * factors[0]
    for k in range(NX - 1):
        merged = merged + ax_dst[k].astype(F32) * factors[k + 1]
    az_src[...] = merged.astype(BF16)
    z_scatter(az_src, az_dst, 8, tz_src, tz_dst, 7)
    drain(tz_dst, recv_sems.at[7])
    own = tz_src[0]
    others = tz_dst[:, 0]
    summit = jnp.maximum(own, jnp.max(others, axis=0))
    own_factor = jnp.exp(own - summit)
    factors = jnp.exp(others - summit)
    total = own_factor * tz_src[1] + jnp.sum(factors * tz_dst[:, 1], axis=0)
    drain(az_dst, recv_sems.at[8])
    merged = own_factor * az_src[mine].astype(F32) + jnp.sum(
        factors * az_dst[...].astype(F32), axis=0
    )
    a_all[slot] = (merged / total).astype(BF16)
    near_gather(a_all, 9)

    loads[5].wait()
    loads[6].wait()
    turned = []
    for j in range(NX):
        block = a_all[CHUNKS * j : CHUNKS * j + CHUNKS].reshape(HD, 128).astype(F32)
        across = jnp.transpose(block).astype(BF16)
        turned += [across[:ROWS], across[ROWS:]]
    projected = jnp.dot(
        jnp.concatenate(turned, axis=1), wout[...], preferred_element_type=F32
    )

    def tp_sum(part, whole, at, sems):
        whole[tp] = part.astype(BF16)
        for k in (4, 5, 2, 3, 6, 7, 1):
            send(whole.at[tp], whole.at[tp], send_sems.at[at], sems.at[tp], (ctx, t_of(k)))
        for k in (1, 7, 6, 3, 2, 5, 4):
            source = t_of(k)
            drain(whole.at[source], sems.at[source])
        at_end(at, whole.at[pl.ds(0, NT - 1)])
        total = whole[0].astype(F32)
        for source in range(1, NT):
            total = total + whole[source].astype(F32)
        return total

    residual = hidden[...].astype(F32) + tp_sum(projected, p_all, 10, p_sems)

    ux_src[...] = lane_row(jnp.sum(residual * residual, axis=1, keepdims=True))
    x_same(ux_src, ux_dst, 11)
    second = (residual * ffn_gain[...]).astype(BF16)
    loads[7].wait()
    loads[8].wait()
    order = FAR_FIRST + (0,)
    for p in range(PIECES):
        for s in range(PIECE):
            block = jnp.minimum(z_of(order[p * PIECE + s]), FF_BLOCKS - 1)
            columns = pl.ds(pl.multiple_of(block * 128, 128), 128)
            pair = jnp.concatenate([wgate[:, columns], wup[:, columns]], axis=1)
            part = jnp.dot(second, pair, preferred_element_type=F32).astype(BF16)
            for j in range(NX):
                fx_src[p, j, s, 0] = part[16 * j : 16 * j + 16, :128]
                fx_src[p, j, s, 1] = part[16 * j : 16 * j + 16, 128:]
        x_scatter(fx_src.at[p], fx_dst.at[p], 12 + p)
    drain(ux_dst, recv_sems.at[11])
    uz_src[...] = ux_src[...] + ux_dst[0] + ux_dst[1] + ux_dst[2]
    for k in FAR_FIRST:
        send(uz_src, uz_dst.at[k - 1], send_sems.at[16], recv_sems.at[16], device(k, 0))
    at_end(16, uz_dst)
    for p in range(PIECES):
        drain(fx_dst.at[p], recv_sems.at[12 + p])
        fz_src[pl.ds(p * PIECE, PIECE)] = (
            fx_src[p, x].astype(F32)
            + fx_dst[p, 0].astype(F32)
            + fx_dst[p, 1].astype(F32)
            + fx_dst[p, 2].astype(F32)
        ).astype(BF16)
        for s in range(PIECE):
            k = order[p * PIECE + s]
            if k == 0:
                continue

            @pl.when(z_of(k) < FF_BLOCKS)
            def _():
                send(
                    fz_src.at[p * PIECE + s],
                    fz_dst.at[k - 1],
                    send_sems.at[17],
                    recv_sems.at[17],
                    device(k, 0),
                )

    reduces = z < FF_BLOCKS
    at_end(17, fz_dst.at[pl.ds(0, FF_BLOCKS - 1)], reduces)
    at_end(17, fz_dst.at[pl.ds(0, FF_BLOCKS)], jnp.logical_not(reduces))
    drain(uz_dst, recv_sems.at[16])
    squares = jnp.sum(uz_dst[...], axis=0) + uz_src[...]
    scale = lax.rsqrt(row_column(squares, 16 * x) / D + EPSILON)

    def x_forward(block):
        for k in (2, 1, 3):
            send(
                f_all.at[x, block],
                f_all.at[x, block],
                send_sems.at[19],
                recv_sems.at[19],
                device(0, k),
            )

    @pl.when(reduces)
    def _():
        drain(fz_dst, recv_sems.at[17])
        both = fz_src[NZ - 1].astype(F32) + jnp.sum(fz_dst[...].astype(F32), axis=0)
        gate = scale * both[0]
        up = scale * both[1]
        f_all[x, z] = (gate / (1.0 + jnp.exp(-gate)) * up).astype(BF16)
        for k in FAR_FIRST:
            send(f_all.at[x, z], f_all.at[x, z], send_sems.at[18], f_gather_sems.at[z], device(k, 0))
        x_forward(z)

    at_end(18, az_dst, reduces)

    for k in reversed(FAR_FIRST):
        block = z_of(k)

        @pl.when(block < FF_BLOCKS)
        def _():
            drain(f_all.at[x, block], f_gather_sems.at[block])
            x_forward(block)

    drain(f_all.at[pl.ds(0, NX - 1)], recv_sems.at[19])
    at_end(19, f_all.at[pl.ds(0, NX - 1)])

    loads[9].wait()
    activated = jnp.concatenate(
        [f_all[:, b].reshape(ROWS, 128) for b in range(FF_BLOCKS)], axis=1
    )
    lowered = jnp.dot(activated, wdown[...], preferred_element_type=F32)
    result = residual + tp_sum(lowered, d_all, 20, d_sems)
    out_ref[...] = result.astype(BF16)
    finish()


def body(
    hidden_in,
    attn_gain,
    w_query,
    key_cache,
    value_cache,
    block_lengths,
    question_length,
    w_out,
    ffn_gain,
    w_gate,
    w_up,
    w_down,
):
    operands = (
        hidden_in,
        attn_gain.reshape(1, -1),
        ffn_gain.reshape(1, -1),
        w_query,
        key_cache,
        value_cache,
        w_out,
        w_gate,
        w_up,
        w_down,
    )
    chunk = (16, 128)
    row = (1, 128)
    dma = pltpu.SemaphoreType.DMA
    scratch = [pltpu.VMEM(a.shape, a.dtype) for a in operands]
    scratch += [dma((len(operands),)), dma((21,)), dma((21,))]
    scratch += [
        pltpu.VMEM((NX, CHUNKS) + chunk, F32),
        pltpu.VMEM((NX - 1, CHUNKS) + chunk, F32),
        pltpu.VMEM((CHUNKS,) + chunk, F32),
        pltpu.VMEM((NZ - 1,) + chunk, F32),
        pltpu.VMEM((NX * CHUNKS,) + chunk, BF16),
        pltpu.VMEM(row, F32),
        pltpu.VMEM((NX - 1,) + row, F32),
        pltpu.VMEM(row, F32),
        pltpu.VMEM((NZ - 1,) + row, F32),
        pltpu.VMEM((NX, CHUNKS) + chunk, BF16),
        pltpu.VMEM((NX - 1, CHUNKS) + chunk, BF16),
        pltpu.VMEM((CHUNKS,) + chunk, BF16),
        pltpu.VMEM((NZ - 1,) + chunk, BF16),
        pltpu.VMEM((NX * CHUNKS,) + chunk, BF16),
        pltpu.VMEM((NX, 2) + row, F32),
        pltpu.VMEM((NX - 1, 2) + row, F32),
        pltpu.VMEM((2,) + row, F32),
        pltpu.VMEM((NZ - 1, 2) + row, F32),
        pltpu.VMEM((NT, ROWS, 128), BF16),
        pltpu.VMEM((PIECES, NX, PIECE, 2) + chunk, BF16),
        pltpu.VMEM((PIECES, NX - 1, PIECE, 2) + chunk, BF16),
        pltpu.VMEM((NZ, 2) + chunk, BF16),
        pltpu.VMEM((NZ - 1, 2) + chunk, BF16),
        pltpu.VMEM((NX, FF_BLOCKS) + chunk, BF16),
        pltpu.VMEM(row, F32),
        pltpu.VMEM((NX - 1,) + row, F32),
        pltpu.VMEM(row, F32),
        pltpu.VMEM((NZ - 1,) + row, F32),
        pltpu.VMEM((NT, ROWS, 128), BF16),
        dma((FF_BLOCKS,)),
        dma((NT,)),
        dma((NT,)),
    ]
    result = pl.pallas_call(
        kernel,
        out_shape=jax.ShapeDtypeStruct(hidden_in.shape, BF16),
        in_specs=[pl.BlockSpec(memory_space=pltpu.SMEM)]
        + [pl.BlockSpec(memory_space=pl.ANY)] * len(operands),
        out_specs=pl.BlockSpec(memory_space=pltpu.VMEM),
        scratch_shapes=scratch,
        compiler_params=pltpu.CompilerParams(
            collective_id=0, has_side_effects=True, vmem_limit_bytes=60 * 1024 * 1024
        ),
    )(block_lengths, *operands)
    present = jnp.arange(ROWS)[:, None] < question_length[0]
    return jnp.where(present, result, jnp.zeros_like(result))


def solution(mesh):
    placed = (
        P(None, "ctx"),
        P("ctx"),
        P("ctx", "tp"),
        P("ctx", "tp"),
        P("ctx", "tp"),
        P("ctx"),
        P(),
        P("tp", "ctx"),
        P("ctx"),
        P("ctx", "tp"),
        P("ctx", "tp"),
        P("tp", "ctx"),
    )
    return jax.shard_map(
        body, mesh=mesh, in_specs=placed, out_specs=P(None, "ctx"), check_vma=False
    )
```

time: 884 us -> 92.3 us (0.10)
  blocking collectives: 425 us -> 0 us
  waiting for transfers between devices: 344 us -> 0 us
  Pallas kernels: 0 us -> 89.3 us
  other arithmetic: 82.2 us -> 1.41 us
  between operations: 14.5 us -> 1.31 us
  matrix products: 10.9 us -> 0 us
    psum x4 -> x0, blocking collectives: 289 us -> none  [the longest x1 123 us: body(): square_sum = lax.psum(square_part, 'ctx')]
    psum x2 -> x0, waiting for transfers between devices: 281 us -> none  [the longest x1 145 us: body(): gate_sum, up_sum = lax.psum((gate_part, up_part), 'ctx')]
    all_gather x2 -> x0, blocking collectives: 136 us -> none  [combined_all(): gathered = jax.tree.map(lambda a: lax.all_gather(a, axis), part)]
    pallas_call x0 -> x1, Pallas kernels: none -> 89.3 us  [body(): pl.pallas_call(kernel, out_shape=jax.ShapeDtypeStruct(hidden_in.shape, BF...]
    add x63 -> x0, other arithmetic: 76.4 us -> none  [combine_pieces(): first[2] * first_factor[..., None] + second[2] * second_factor[..., None]]
    all_gather x1 -> x0, waiting for transfers between devices: 63.4 us -> none  [combined_all(): gathered = jax.tree.map(lambda a: lax.all_gather(a, axis), part)]
    dot_general x7 -> x0, matrix products: 10.9 us -> none  [the longest x1 2.03 us: body(): jnp.dot(second_normed, w_gate, preferred_element_type=jnp.float32)]
  transfers between devices with their start and end apart: 3 -> 0, of which waited for: 3 -> 0; matrix products, arithmetic and copies ran while one was open for 0% -> 0% of each run, Pallas kernels for 0% -> 0%
where the time goes in v2:
time: 92.3 us; the launch traced here: 92 us
  Pallas kernels  89.3 us (97%)
  other arithmetic  1.41 us (2%)
  between operations  1.31 us (1%)
    pallas_call x1, Pallas kernels, body(): pl.pallas_call(kernel, out_shape=jax.ShapeDtypeStruct(hidden_in.shape, BF...  89.3 us

profile of v2, /device:TPU:1, one launch (start us, length us, event | category | flops | bytes accessed | tf_op | source)
XLA Modules:
  0.0 92.0 jit_solution(5406009384196985104)
XLA Ops:
  1.3 89.3 %shard_map.118 = bf16[64,128]{1,0:T(8,128)(2,1)} custom-call(s32[1]{0:T(128)S(6)} %copy.13.length_ref, bf16[64,128]{1,0:T(8,128)(2,1)} %hidden_hbm.1, f32[1,128]{1,0:T(1,128)} %bitcast.4, f32[1,128]{1,0:T(1,128)} %bitcast.5, bf16[128,1024]{1,0:T(8,128)(2,1)} %wq_hbm.1, bf16[512,128]{1,0:T(8,128)(2,1)} %key_hbm.1, bf16[512,128]{1,0:T(8,128)(2,1)} %value_hbm.1, ...), custom_call_target="tpu_custom_call" | custom-call | tf_op jit(solution)/shard_map/pallas_call | solution.py:495
  90.6 1.4 %broadcast_select_fusion = bf16[64,128]{1,0:T(8,128)(2,1)} fusion(bf16[64,128]{1,0:T(8,128)(2,1)} %shard_map.118, pred[64]{0:T(512)(128)(4,1)S(1)} %iota_compare_fusion), kind=kLoop, calls=%fused_computation | loop fusion | flops 8192 | bytes 32832 | tf_op jit(solution)/shard_map/jit(_where)/select_n | solution.py:507
  (1 shorter events, 0.0 us)

commit v3 on v2

--- a/solution.py
+++ b/solution.py
@@ -16,19 +16,20 @@
 NZ = 16
 NT = 8
 ROWS = 64
+BLOCK = 512
 CHUNKS = 8
 FF_BLOCKS = 14
 PIECES = 4
 PIECE = NZ // PIECES
 FAR_FIRST = (8, 7, 9, 6, 10, 5, 11, 4, 12, 3, 13, 2, 14, 1, 15)
+QUERY_OFFSETS = ((8, 7, 9, 6, 14, 1, 15), (10, 5, 11, 4, 12, 3, 13, 2))
+NEAR_Z = (4, 3, 13, 2, 14, 1, 15)
 NEAR = tuple(
     (dz % NZ, dx)
     for dz in (4, 3, -3, 2, -2, 1, -1, 0)
     for dx in (2, 1, 3, 0)
     if (dz, dx) != (0, 0)
 )
-NEAR_ONE_WAY = tuple((dz, dx) for dz, dx in NEAR if dz == 4 and dx != 0)
-PARTNERS = NX - 1 + NZ - 1 + NT - 1 + 7 * 3 + 3
 MESH = pl.DeviceIdType.MESH
 F32 = jnp.float32
 BF16 = jnp.bfloat16
@@ -83,13 +84,15 @@
     sx_dst,
     sz_src,
     sz_dst,
-    ax_src,
-    ax_dst,
+    kx_dst,
+    vx_dst,
+    lx_src,
+    lx_dst,
+    v_turned,
+    w_turned,
     az_src,
     az_dst,
     a_all,
-    tx_src,
-    tx_dst,
     tz_src,
     tz_dst,
     p_all,
@@ -103,6 +106,7 @@
     uz_src,
     uz_dst,
     d_all,
+    word_sems,
     f_gather_sems,
     p_sems,
     d_sems,
@@ -145,21 +149,22 @@
         load.start()
 
     barrier = pltpu.get_barrier_semaphore()
-
-    def greet(peer):
-        pl.semaphore_signal(barrier, inc=1, device_id=peer, device_id_type=MESH)
-
-    for k in FAR_FIRST:
-        greet(device(k, 0))
+    for k in (2, 14, 1, 15):
+        pl.semaphore_signal(barrier, inc=1, device_id=device(k, 0), device_id_type=MESH)
     for k in range(1, NX):
-        greet(device(0, k))
+        pl.semaphore_signal(barrier, inc=1, device_id=device(0, k), device_id_type=MESH)
     for k in range(1, NT):
-        greet((ctx, t_of(k)))
-    for dz, dx in NEAR:
-        if dz != 0 and dx != 0:
-            greet(device(dz, dx))
-    for dz, dx in NEAR_ONE_WAY:
-        greet(device(-dz % NZ, -dx % NX))
+        pl.semaphore_signal(barrier, inc=1, device_id=(ctx, t_of(k)), device_id_type=MESH)
+
+    def pass_on(step):
+        for k in (step, NZ - step):
+            pl.semaphore_signal(
+                word_sems.at[step // 4], inc=1, device_id=device(k, 0), device_id_type=MESH
+            )
+
+    def word(step):
+        pl.semaphore_wait(word_sems.at[step // 4], 2)
+
     for load in loads[3:]:
         load.start()
 
@@ -232,90 +237,112 @@
     normed = (stream * attn_gain[...]).astype(BF16)
     loads[2].wait()
     query_part = jnp.dot(normed, wq[...], preferred_element_type=F32)
+    for i in range(CHUNKS):
+        place = lax.rem(i - z + NZ + 2, CHUNKS)
+        for j in range(NX):
+            column = (2 * j + i // 4) * HD
+            row = 16 * (i % 4)
+            qx_src[lax.div(place, 4), j, lax.rem(place, 4)] = query_part[
+                row : row + 16, column : column + HD
+            ]
+    pl.semaphore_wait(barrier, 4 + NX - 1 + NT - 1)
+    pass_on(2)
+
+    x_same(sx_src, sx_dst, 0)
+    for p in range(2):
+        x_scatter(qx_src.at[p], qx_dst.at[p], 1 + p)
+    word(2)
+    pass_on(4)
+    loads[3].wait()
+    loads[4].wait()
+    lx_src[...] = jnp.full((1, 128), length_ref[0].astype(F32), F32)
+    drain(sx_dst, recv_sems.at[0])
+    sz_src[...] = sx_src[...] + sx_dst[0] + sx_dst[1] + sx_dst[2]
+    word(4)
+    for p, offsets in enumerate(QUERY_OFFSETS):
+        drain(qx_dst.at[p], recv_sems.at[1 + p])
+        qz_src[pl.ds(4 * p, 4)] = qx_src[p, x] + qx_dst[p, 0] + qx_dst[p, 1] + qx_dst[p, 2]
+        for k in offsets:
+            send(sz_src, sz_dst.at[k - 1], send_sems.at[3], recv_sems.at[3], device(k, 0))
+            send(
+                qz_src.at[(k + 2) % CHUNKS],
+                qz_dst.at[k - 1],
+                send_sems.at[4],
+                recv_sems.at[4],
+                device(k, 0),
+            )
+    at_end(3, sz_dst)
+    at_end(4, qz_dst)
+    x_same(lx_src, lx_dst, 5)
+    x_same(key, kx_dst, 6)
+    x_same(value, vx_dst, 7)
+    mine = lax.rem(z, CHUNKS)
+    slot = x * CHUNKS + mine
+    drain(sz_dst, recv_sems.at[3])
+    squares = jnp.sum(sz_dst[...], axis=0) + sz_src[...]
+    scale = lax.rsqrt(row_column(squares, 16 * lax.rem(mine, 4)) / D + EPSILON)
+    drain(qz_dst, recv_sems.at[4])
+    total = qz_src[2] + jnp.sum(qz_dst[...], axis=0)
+    q_all[mine] = (scale * total).astype(BF16)
+    for dz in NEAR_Z:
+        send(q_all.at[mine], q_all.at[mine], send_sems.at[8], recv_sems.at[8], device(dz, 0))
+    at_end(8, q_all.at[pl.ds(0, CHUNKS - 1)])
+    loads[6].wait()
     for j in range(NX):
         for h in range(2):
-            for g in range(4):
-                column = (2 * j + h) * HD
-                qx_src[j, 4 * h + g] = query_part[16 * g : 16 * g + 16, column : column + HD]
-    pl.semaphore_wait(barrier, PARTNERS)
-
-    x_same(sx_src, sx_dst, 0)
-    x_scatter(qx_src, qx_dst, 1)
-    drain(sx_dst, recv_sems.at[0])
-    sz_src[...] = sx_src[...] + sx_dst[0] + sx_dst[1] + sx_dst[2]
-    drain(qx_dst, recv_sems.at[1])
-    qz_src[...] = qx_src[x] + qx_dst[0] + qx_dst[1] + qx_dst[2]
-    z_scatter(qz_src, qz_dst, 3, sz_src, sz_dst, 2)
-    mine = lax.rem(z, CHUNKS)
-    slot = x * CHUNKS + mine
-    drain(sz_dst, recv_sems.at[2])
-    squares = jnp.sum(sz_dst[...], axis=0) + sz_src[...]
-    scale = lax.rsqrt(row_column(squares, 16 * lax.rem(mine, 4)) / D + EPSILON)
-    drain(qz_dst, recv_sems.at[3])
-    total = qz_src[mine] + jnp.sum(qz_dst[...], axis=0)
-    q_all[slot] = (scale * total).astype(BF16)
-    near_gather(q_all, 4)
-
-    loads[3].wait()
-    loads[4].wait()
-    queries = q_all[...].reshape(NX * CHUNKS * 16, HD)
-    scores = lax.dot_general(
-        key[...], queries, (((1,), (1,)), ((), ())), preferred_element_type=F32
-    ) * (1.0 / math.sqrt(HD))
-    usable = lax.broadcasted_iota(jnp.int32, scores.shape, 0) < length_ref[0]
-    scores = jnp.where(usable, scores, MASKED)
-    maxima = jnp.max(scores, axis=0, keepdims=True)
-    weights = jnp.exp(scores - maxima)
-    totals = jnp.sum(weights, axis=0, keepdims=True)
-    for j in range(NX):
-        tx_src[j, 0] = maxima[:, 128 * j : 128 * j + 128]
-        tx_src[j, 1] = totals[:, 128 * j : 128 * j + 128]
-    x_scatter(tx_src, tx_dst, 5)
-    numerators = lax.dot_general(
-        value[...], weights.astype(BF16), (((0,), (0,)), ((), ())), preferred_element_type=F32
-    ).astype(BF16)
-    for j in range(NX):
-        for i in range(CHUNKS):
-            ax_src[j, i] = numerators[16 * i : 16 * i + 16, 128 * j : 128 * j + 128]
-    x_scatter(ax_src, ax_dst, 6)
-    drain(tx_dst, recv_sems.at[5])
-    pieces = [tx_src.at[x]] + [tx_dst.at[k] for k in range(NX - 1)]
-    summit = pieces[0][0]
-    for piece in pieces[1:]:
-        summit = jnp.maximum(summit, piece[0])
-    factors = [jnp.exp(piece[0] - summit) for piece in pieces]
+            at = (2 * j + h) * HD
+            w_turned[pl.ds(HD * h, HD), pl.ds(HD * j, HD)] = jnp.transpose(
+                wout[at : at + HD].astype(F32)
+            ).astype(BF16)
+    drain(lx_dst, recv_sems.at[5])
+    drain(kx_dst, recv_sems.at[6])
+    drain(vx_dst, recv_sems.at[7])
+    keys = [key] + [kx_dst.at[k] for k in range(NX - 1)]
+    values = [value] + [vx_dst.at[k] for k in range(NX - 1)]
+    lengths = [lx_src] + [lx_dst.at[k] for k in range(NX - 1)]
+    for n in range(NX):
+        v_turned[n] = jnp.transpose(values[n][...].astype(F32)).astype(BF16)
+    drain(q_all.at[pl.ds(0, CHUNKS - 1)], recv_sems.at[8])
+
+    queries = q_all[...].reshape(CHUNKS * 16, HD)
+    token = lax.broadcasted_iota(jnp.int32, (BLOCK, 128), 0).astype(F32)
+    found = []
+    for n in range(NX):
+        scores = lax.dot_general(
+            keys[n][...], queries, (((1,), (1,)), ((), ())), preferred_element_type=F32
+        ) * (1.0 / math.sqrt(HD))
+        scores = jnp.where(token < lengths[n][...], scores, MASKED)
+        maxima = jnp.max(scores, axis=0, keepdims=True)
+        weights = jnp.exp(scores - maxima)
+        totals = jnp.sum(weights, axis=0, keepdims=True)
+        numerators = jnp.dot(v_turned[n], weights.astype(BF16), preferred_element_type=F32)
+        found.append((maxima, totals, numerators))
+    summit = functools.reduce(jnp.maximum, [piece[0] for piece in found])
+    factors = [jnp.exp(piece[0] - summit) for piece in found]
     tz_src[0] = summit
-    tz_src[1] = sum(factor * piece[1] for factor, piece in zip(factors, pieces))
-    drain(ax_dst, recv_sems.at[6])
-    merged = ax_src[x].astype(F32) * factors[0]
-    for k in range(NX - 1):
-        merged = merged + ax_dst[k].astype(F32) * factors[k + 1]
-    az_src[...] = merged.astype(BF16)
-    z_scatter(az_src, az_dst, 8, tz_src, tz_dst, 7)
-    drain(tz_dst, recv_sems.at[7])
+    tz_src[1] = sum(factor * piece[1] for factor, piece in zip(factors, found))
+    merged = sum(factor * piece[2] for factor, piece in zip(factors, found))
+    for i in range(CHUNKS):
+        az_src[i] = merged[16 * i : 16 * i + 16].astype(BF16)
+    z_scatter(az_src, az_dst, 10, tz_src, tz_dst, 9)
+    drain(tz_dst, recv_sems.at[9])
     own = tz_src[0]
     others = tz_dst[:, 0]
     summit = jnp.maximum(own, jnp.max(others, axis=0))
     own_factor = jnp.exp(own - summit)
     factors = jnp.exp(others - summit)
     total = own_factor * tz_src[1] + jnp.sum(factors * tz_dst[:, 1], axis=0)
-    drain(az_dst, recv_sems.at[8])
+    drain(az_dst, recv_sems.at[10])
     merged = own_factor * az_src[mine].astype(F32) + jnp.sum(
         factors * az_dst[...].astype(F32), axis=0
     )
     a_all[slot] = (merged / total).astype(BF16)
-    near_gather(a_all, 9)
-
-    loads[5].wait()
-    loads[6].wait()
-    turned = []
-    for j in range(NX):
-        block = a_all[CHUNKS * j : CHUNKS * j + CHUNKS].reshape(HD, 128).astype(F32)
-        across = jnp.transpose(block).astype(BF16)
-        turned += [across[:ROWS], across[ROWS:]]
-    projected = jnp.dot(
-        jnp.concatenate(turned, axis=1), wout[...], preferred_element_type=F32
-    )
+    near_gather(a_all, 11)
+
+    both = jnp.dot(
+        w_turned[...], a_all[...].reshape(NX * HD, 128), preferred_element_type=F32
+    )
+    projected = jnp.transpose(both[:HD, :ROWS] + both[HD:, ROWS:])
 
     def tp_sum(part, whole, at, sems):
         whole[tp] = part.astype(BF16)
@@ -330,10 +357,11 @@
             total = total + whole[source].astype(F32)
         return total
 
-    residual = hidden[...].astype(F32) + tp_sum(projected, p_all, 10, p_sems)
-
+    residual = hidden[...].astype(F32) + tp_sum(projected, p_all, 12, p_sems)
+
+    loads[5].wait()
     ux_src[...] = lane_row(jnp.sum(residual * residual, axis=1, keepdims=True))
-    x_same(ux_src, ux_dst, 11)
+    x_same(ux_src, ux_dst, 13)
     second = (residual * ffn_gain[...]).astype(BF16)
     loads[7].wait()
     loads[8].wait()
@@ -347,14 +375,14 @@
             for j in range(NX):
                 fx_src[p, j, s, 0] = part[16 * j : 16 * j + 16, :128]
                 fx_src[p, j, s, 1] = part[16 * j : 16 * j + 16, 128:]
-        x_scatter(fx_src.at[p], fx_dst.at[p], 12 + p)
-    drain(ux_dst, recv_sems.at[11])
+        x_scatter(fx_src.at[p], fx_dst.at[p], 14 + p)
+    drain(ux_dst, recv_sems.at[13])
     uz_src[...] = ux_src[...] + ux_dst[0] + ux_dst[1] + ux_dst[2]
     for k in FAR_FIRST:
-        send(uz_src, uz_dst.at[k - 1], send_sems.at[16], recv_sems.at[16], device(k, 0))
-    at_end(16, uz_dst)
+        send(uz_src, uz_dst.at[k - 1], send_sems.at[18], recv_sems.at[18], device(k, 0))
+    at_end(18, uz_dst)
     for p in range(PIECES):
-        drain(fx_dst.at[p], recv_sems.at[12 + p])
+        drain(fx_dst.at[p], recv_sems.at[14 + p])
         fz_src[pl.ds(p * PIECE, PIECE)] = (
             fx_src[p, x].astype(F32)
             + fx_dst[p, 0].astype(F32)
@@ -371,15 +399,15 @@
                 send(
                     fz_src.at[p * PIECE + s],
                     fz_dst.at[k - 1],
-                    send_sems.at[17],
-                    recv_sems.at[17],
+                    send_sems.at[19],
+                    recv_sems.at[19],
                     device(k, 0),
                 )
 
     reduces = z < FF_BLOCKS
-    at_end(17, fz_dst.at[pl.ds(0, FF_BLOCKS - 1)], reduces)
-    at_end(17, fz_dst.at[pl.ds(0, FF_BLOCKS)], jnp.logical_not(reduces))
-    drain(uz_dst, recv_sems.at[16])
+    at_end(19, fz_dst.at[pl.ds(0, FF_BLOCKS - 1)], reduces)
+    at_end(19, fz_dst.at[pl.ds(0, FF_BLOCKS)], jnp.logical_not(reduces))
+    drain(uz_dst, recv_sems.at[18])
     squares = jnp.sum(uz_dst[...], axis=0) + uz_src[...]
     scale = lax.rsqrt(row_column(squares, 16 * x) / D + EPSILON)
 
@@ -388,23 +416,23 @@
             send(
                 f_all.at[x, block],
                 f_all.at[x, block],
-                send_sems.at[19],
-                recv_sems.at[19],
+                send_sems.at[21],
+                recv_sems.at[21],
                 device(0, k),
             )
 
     @pl.when(reduces)
     def _():
-        drain(fz_dst, recv_sems.at[17])
+        drain(fz_dst, recv_sems.at[19])
         both = fz_src[NZ - 1].astype(F32) + jnp.sum(fz_dst[...].astype(F32), axis=0)
         gate = scale * both[0]
         up = scale * both[1]
         f_all[x, z] = (gate / (1.0 + jnp.exp(-gate)) * up).astype(BF16)
         for k in FAR_FIRST:
-            send(f_all.at[x, z], f_all.at[x, z], send_sems.at[18], f_gather_sems.at[z], device(k, 0))
+            send(f_all.at[x, z], f_all.at[x, z], send_sems.at[20], f_gather_sems.at[z], device(k, 0))
         x_forward(z)
 
-    at_end(18, az_dst, reduces)
+    at_end(20, az_dst, reduces)
 
     for k in reversed(FAR_FIRST):
         block = z_of(k)
@@ -414,15 +442,15 @@
             drain(f_all.at[x, block], f_gather_sems.at[block])
             x_forward(block)
 
-    drain(f_all.at[pl.ds(0, NX - 1)], recv_sems.at[19])
-    at_end(19, f_all.at[pl.ds(0, NX - 1)])
+    drain(f_all.at[pl.ds(0, NX - 1)], recv_sems.at[21])
+    at_end(21, f_all.at[pl.ds(0, NX - 1)])
 
     loads[9].wait()
     activated = jnp.concatenate(
         [f_all[:, b].reshape(ROWS, 128) for b in range(FF_BLOCKS)], axis=1
     )
     lowered = jnp.dot(activated, wdown[...], preferred_element_type=F32)
-    result = residual + tp_sum(lowered, d_all, 20, d_sems)
+    result = residual + tp_sum(lowered, d_all, 22, d_sems)
     out_ref[...] = result.astype(BF16)
     finish()
 
@@ -457,24 +485,26 @@
     row = (1, 128)
     dma = pltpu.SemaphoreType.DMA
     scratch = [pltpu.VMEM(a.shape, a.dtype) for a in operands]
-    scratch += [dma((len(operands),)), dma((21,)), dma((21,))]
+    scratch += [dma((len(operands),)), dma((23,)), dma((23,))]
     scratch += [
-        pltpu.VMEM((NX, CHUNKS) + chunk, F32),
-        pltpu.VMEM((NX - 1, CHUNKS) + chunk, F32),
+        pltpu.VMEM((2, NX, 4) + chunk, F32),
+        pltpu.VMEM((2, NX - 1, 4) + chunk, F32),
         pltpu.VMEM((CHUNKS,) + chunk, F32),
         pltpu.VMEM((NZ - 1,) + chunk, F32),
-        pltpu.VMEM((NX * CHUNKS,) + chunk, BF16),
+        pltpu.VMEM((CHUNKS,) + chunk, BF16),
         pltpu.VMEM(row, F32),
         pltpu.VMEM((NX - 1,) + row, F32),
         pltpu.VMEM(row, F32),
         pltpu.VMEM((NZ - 1,) + row, F32),
-        pltpu.VMEM((NX, CHUNKS) + chunk, BF16),
-        pltpu.VMEM((NX - 1, CHUNKS) + chunk, BF16),
+        pltpu.VMEM((NX - 1, BLOCK, HD), BF16),
+        pltpu.VMEM((NX - 1, BLOCK, HD), BF16),
+        pltpu.VMEM(row, F32),
+        pltpu.VMEM((NX - 1,) + row, F32),
+        pltpu.VMEM((NX, HD, BLOCK), BF16),
+        pltpu.VMEM((2 * HD, NX * HD), BF16),
         pltpu.VMEM((CHUNKS,) + chunk, BF16),
         pltpu.VMEM((NZ - 1,) + chunk, BF16),
         pltpu.VMEM((NX * CHUNKS,) + chunk, BF16),
-        pltpu.VMEM((NX, 2) + row, F32),
-        pltpu.VMEM((NX - 1, 2) + row, F32),
         pltpu.VMEM((2,) + row, F32),
         pltpu.VMEM((NZ - 1, 2) + row, F32),
         pltpu.VMEM((NT, ROWS, 128), BF16),
@@ -488,6 +518,7 @@
         pltpu.VMEM(row, F32),
         pltpu.VMEM((NZ - 1,) + row, F32),
         pltpu.VMEM((NT, ROWS, 128), BF16),
+        pltpu.SemaphoreType.REGULAR((2,)),
         dma((FF_BLOCKS,)),
         dma((NT,)),
         dma((NT,)),

time: 92.3 us -> 85.3 us (0.924)
  Pallas kernels: 89.3 us -> 82.3 us
    pallas_call x1, Pallas kernels: 89.3 us -> 82.3 us  [body(): pl.pallas_call(kernel, out_shape=jax.ShapeDtypeStruct(hidden_in.shape, BF...]
where the time goes in v3:
time: 85.3 us; the launch traced here: 85 us
  Pallas kernels  82.3 us (96%)
  other arithmetic  1.41 us (2%)
  between operations  1.31 us (2%)
    pallas_call x1, Pallas kernels, body(): pl.pallas_call(kernel, out_shape=jax.ShapeDtypeStruct(hidden_in.shape, BF...  82.3 us

profile of v3, /device:TPU:1, one launch (start us, length us, event | category | flops | bytes accessed | tf_op | source)
XLA Modules:
  0.0 85.0 jit_solution(7854009538814398802)
XLA Ops:
  1.3 82.3 %shard_map.118 = bf16[64,128]{1,0:T(8,128)(2,1)} custom-call(s32[1]{0:T(128)S(6)} %copy.13.length_ref, bf16[64,128]{1,0:T(8,128)(2,1)} %hidden_hbm.1, f32[1,128]{1,0:T(1,128)} %bitcast.4, f32[1,128]{1,0:T(1,128)} %bitcast.5, bf16[128,1024]{1,0:T(8,128)(2,1)} %wq_hbm.1, bf16[512,128]{1,0:T(8,128)(2,1)} %key_hbm.1, bf16[512,128]{1,0:T(8,128)(2,1)} %value_hbm.1, ...), custom_call_target="tpu_custom_call" | custom-call | tf_op jit(solution)/shard_map/pallas_call | solution.py:526
  83.6 1.4 %broadcast_select_fusion = bf16[64,128]{1,0:T(8,128)(2,1)} fusion(bf16[64,128]{1,0:T(8,128)(2,1)} %shard_map.118, pred[64]{0:T(512)(128)(4,1)S(1)} %iota_compare_fusion), kind=kLoop, calls=%fused_computation | loop fusion | flops 8192 | bytes 32832 | tf_op jit(solution)/shard_map/jit(_where)/select_n | solution.py:538
  (1 shorter events, 0.0 us)

commit v4 on v3

--- a/solution.py
+++ b/solution.py
@@ -12,6 +12,7 @@
 HD = 128
 EPSILON = 1e-05
 MASKED = -1e30
+LAST = 22
 NX = 4
 NZ = 16
 NT = 8
@@ -19,8 +20,7 @@
 BLOCK = 512
 CHUNKS = 8
 FF_BLOCKS = 14
-PIECES = 4
-PIECE = NZ // PIECES
+PIECES = ((0, 2), (2, 3), (5, 5), (10, 6))
 FAR_FIRST = (8, 7, 9, 6, 10, 5, 11, 4, 12, 3, 13, 2, 14, 1, 15)
 QUERY_OFFSETS = ((8, 7, 9, 6, 14, 1, 15), (10, 5, 11, 4, 12, 3, 13, 2))
 NEAR_Z = (4, 3, 13, 2, 14, 1, 15)
@@ -145,9 +145,6 @@
         pltpu.make_async_copy(source, target, load_sems.at[at])
         for at, (source, target) in enumerate(zip(sources, targets))
     ]
-    for load in loads[:3]:
-        load.start()
-
     barrier = pltpu.get_barrier_semaphore()
     for k in (2, 14, 1, 15):
         pl.semaphore_signal(barrier, inc=1, device_id=device(k, 0), device_id_type=MESH)
@@ -156,6 +153,9 @@
     for k in range(1, NT):
         pl.semaphore_signal(barrier, inc=1, device_id=(ctx, t_of(k)), device_id_type=MESH)
 
+    for load in loads:
+        load.start()
+
     def pass_on(step):
         for k in (step, NZ - step):
             pl.semaphore_signal(
@@ -164,9 +164,6 @@
 
     def word(step):
         pl.semaphore_wait(word_sems.at[step // 4], 2)
-
-    for load in loads[3:]:
-        load.start()
 
     def send(source, target, send_sem, recv_sem, peer):
         pltpu.make_async_remote_copy(
@@ -233,7 +230,6 @@
     loads[0].wait()
     loads[1].wait()
     stream = hidden[...].astype(F32)
-    sx_src[...] = lane_row(jnp.sum(stream * stream, axis=1, keepdims=True))
     normed = (stream * attn_gain[...]).astype(BF16)
     loads[2].wait()
     query_part = jnp.dot(normed, wq[...], preferred_element_type=F32)
@@ -248,22 +244,20 @@
     pl.semaphore_wait(barrier, 4 + NX - 1 + NT - 1)
     pass_on(2)
 
-    x_same(sx_src, sx_dst, 0)
     for p in range(2):
         x_scatter(qx_src.at[p], qx_dst.at[p], 1 + p)
+    sx_src[...] = lane_row(jnp.sum(stream * stream, axis=1, keepdims=True))
+    x_same(sx_src, sx_dst, 0)
     word(2)
     pass_on(4)
     loads[3].wait()
     loads[4].wait()
     lx_src[...] = jnp.full((1, 128), length_ref[0].astype(F32), F32)
-    drain(sx_dst, recv_sems.at[0])
-    sz_src[...] = sx_src[...] + sx_dst[0] + sx_dst[1] + sx_dst[2]
     word(4)
     for p, offsets in enumerate(QUERY_OFFSETS):
         drain(qx_dst.at[p], recv_sems.at[1 + p])
         qz_src[pl.ds(4 * p, 4)] = qx_src[p, x] + qx_dst[p, 0] + qx_dst[p, 1] + qx_dst[p, 2]
         for k in offsets:
-            send(sz_src, sz_dst.at[k - 1], send_sems.at[3], recv_sems.at[3], device(k, 0))
             send(
                 qz_src.at[(k + 2) % CHUNKS],
                 qz_dst.at[k - 1],
@@ -271,7 +265,12 @@
                 recv_sems.at[4],
                 device(k, 0),
             )
-    at_end(3, sz_dst)
+        if p == 0:
+            drain(sx_dst, recv_sems.at[0])
+            sz_src[...] = sx_src[...] + sx_dst[0] + sx_dst[1] + sx_dst[2]
+            for k in FAR_FIRST:
+                send(sz_src, sz_dst.at[k - 1], send_sems.at[3], recv_sems.at[3], device(k, 0))
+            at_end(3, sz_dst)
     at_end(4, qz_dst)
     x_same(lx_src, lx_dst, 5)
     x_same(key, kx_dst, 6)
@@ -348,10 +347,15 @@
         whole[tp] = part.astype(BF16)
         for k in (4, 5, 2, 3, 6, 7, 1):
             send(whole.at[tp], whole.at[tp], send_sems.at[at], sems.at[tp], (ctx, t_of(k)))
+        if at == LAST:
+            finish()
         for k in (1, 7, 6, 3, 2, 5, 4):
             source = t_of(k)
             drain(whole.at[source], sems.at[source])
-        at_end(at, whole.at[pl.ds(0, NT - 1)])
+        if at == LAST:
+            drain(whole.at[pl.ds(0, NT - 1)], send_sems.at[at])
+        else:
+            at_end(at, whole.at[pl.ds(0, NT - 1)])
         total = whole[0].astype(F32)
         for source in range(1, NT):
             total = total + whole[source].astype(F32)
@@ -360,44 +364,54 @@
     residual = hidden[...].astype(F32) + tp_sum(projected, p_all, 12, p_sems)
 
     loads[5].wait()
-    ux_src[...] = lane_row(jnp.sum(residual * residual, axis=1, keepdims=True))
-    x_same(ux_src, ux_dst, 13)
     second = (residual * ffn_gain[...]).astype(BF16)
     loads[7].wait()
     loads[8].wait()
     order = FAR_FIRST + (0,)
-    for p in range(PIECES):
-        for s in range(PIECE):
-            block = jnp.minimum(z_of(order[p * PIECE + s]), FF_BLOCKS - 1)
+    ux_row = lane_row(jnp.sum(residual * residual, axis=1, keepdims=True))
+    for p, (start, size) in enumerate(PIECES):
+        for s in range(size):
+            block = jnp.minimum(z_of(order[start + s]), FF_BLOCKS - 1)
             columns = pl.ds(pl.multiple_of(block * 128, 128), 128)
             pair = jnp.concatenate([wgate[:, columns], wup[:, columns]], axis=1)
             part = jnp.dot(second, pair, preferred_element_type=F32).astype(BF16)
             for j in range(NX):
-                fx_src[p, j, s, 0] = part[16 * j : 16 * j + 16, :128]
-                fx_src[p, j, s, 1] = part[16 * j : 16 * j + 16, 128:]
-        x_scatter(fx_src.at[p], fx_dst.at[p], 14 + p)
-    drain(ux_dst, recv_sems.at[13])
-    uz_src[...] = ux_src[...] + ux_dst[0] + ux_dst[1] + ux_dst[2]
-    for k in FAR_FIRST:
-        send(uz_src, uz_dst.at[k - 1], send_sems.at[18], recv_sems.at[18], device(k, 0))
-    at_end(18, uz_dst)
-    for p in range(PIECES):
-        drain(fx_dst.at[p], recv_sems.at[14 + p])
-        fz_src[pl.ds(p * PIECE, PIECE)] = (
-            fx_src[p, x].astype(F32)
-            + fx_dst[p, 0].astype(F32)
-            + fx_dst[p, 1].astype(F32)
-            + fx_dst[p, 2].astype(F32)
-        ).astype(BF16)
-        for s in range(PIECE):
-            k = order[p * PIECE + s]
+                fx_src[NX * start + j * size + s, 0] = part[16 * j : 16 * j + 16, :128]
+                fx_src[NX * start + j * size + s, 1] = part[16 * j : 16 * j + 16, 128:]
+        for k in range(1, NX):
+            send(
+                fx_src.at[pl.ds(NX * start + x_of(k) * size, size)],
+                fx_dst.at[pl.ds((NX - 1) * start + (k - 1) * size, size)],
+                send_sems.at[14 + p],
+                recv_sems.at[14 + p],
+                device(0, k),
+            )
+        at_end(14 + p, fx_dst.at[pl.ds((NX - 1) * start, (NX - 1) * size)])
+        if p == 0:
+            ux_src[...] = ux_row
+            x_same(ux_src, ux_dst, 13)
+    for p, (start, size) in enumerate(PIECES):
+        drain(fx_dst.at[pl.ds((NX - 1) * start, (NX - 1) * size)], recv_sems.at[14 + p])
+        piece = fx_src[pl.ds(NX * start + x * size, size)].astype(F32)
+        for k in range(1, NX):
+            at = (NX - 1) * start + (k - 1) * size
+            piece = piece + fx_dst[at : at + size].astype(F32)
+        fz_src[start : start + size] = piece.astype(BF16)
+        if p == 1:
+            drain(ux_dst, recv_sems.at[13])
+            uz_src[...] = ux_src[...] + ux_dst[0] + ux_dst[1] + ux_dst[2]
+            for k in FAR_FIRST:
+                send(uz_src, uz_dst.at[k - 1], send_sems.at[18], recv_sems.at[18], device(k, 0))
+            at_end(18, uz_dst)
+        for s in range(size):
+            k = order[start + s]
             if k == 0:
                 continue
 
             @pl.when(z_of(k) < FF_BLOCKS)
             def _():
                 send(
-                    fz_src.at[p * PIECE + s],
+                    fz_src.at[start + s],
                     fz_dst.at[k - 1],
                     send_sems.at[19],
                     recv_sems.at[19],
@@ -452,7 +466,6 @@
     lowered = jnp.dot(activated, wdown[...], preferred_element_type=F32)
     result = residual + tp_sum(lowered, d_all, 22, d_sems)
     out_ref[...] = result.astype(BF16)
-    finish()
 
 
 def body(
@@ -508,8 +521,8 @@
         pltpu.VMEM((2,) + row, F32),
         pltpu.VMEM((NZ - 1, 2) + row, F32),
         pltpu.VMEM((NT, ROWS, 128), BF16),
-        pltpu.VMEM((PIECES, NX, PIECE, 2) + chunk, BF16),
-        pltpu.VMEM((PIECES, NX - 1, PIECE, 2) + chunk, BF16),
+        pltpu.VMEM((NX * NZ, 2) + chunk, BF16),
+        pltpu.VMEM(((NX - 1) * NZ, 2) + chunk, BF16),
         pltpu.VMEM((NZ, 2) + chunk, BF16),
         pltpu.VMEM((NZ - 1, 2) + chunk, BF16),
         pltpu.VMEM((NX, FF_BLOCKS) + chunk, BF16),
@@ -525,7 +538,7 @@
     ]
     result = pl.pallas_call(
         kernel,
-        out_shape=jax.ShapeDtypeStruct(hidden_in.shape, BF16),
+        out_shape=pltpu.VMEM(hidden_in.shape, BF16),
         in_specs=[pl.BlockSpec(memory_space=pltpu.SMEM)]
         + [pl.BlockSpec(memory_space=pl.ANY)] * len(operands),
         out_specs=pl.BlockSpec(memory_space=pltpu.VMEM),

time: 85.3 us -> 83.8 us (0.982)
  no operation moved by 1% of the time
where the time goes in v4:
time: 83.8 us; the launch traced here: 83.6 us
  Pallas kernels  81.6 us (97%)
  between operations  1.31 us (2%)
    pallas_call x1, Pallas kernels, body(): pl.pallas_call(kernel, out_shape=pltpu.VMEM(hidden_in.shape, BF16), in_sp...  81.6 us

profile of v4, /device:TPU:1, one launch (start us, length us, event | category | flops | bytes accessed | tf_op | source)
XLA Modules:
  0.0 83.6 jit_solution(15456673303269815840)
XLA Ops:
  1.3 81.6 %shard_map.118 = bf16[64,128]{1,0:T(8,128)(2,1)S(1)} custom-call(s32[1]{0:T(128)S(6)} %copy.13.length_ref, bf16[64,128]{1,0:T(8,128)(2,1)} %hidden_hbm.1, f32[1,128]{1,0:T(1,128)} %bitcast.4, f32[1,128]{1,0:T(1,128)} %bitcast.5, bf16[128,1024]{1,0:T(8,128)(2,1)} %wq_hbm.1, bf16[512,128]{1,0:T(8,128)(2,1)} %key_hbm.1, bf16[512,128]{1,0:T(8,128)(2,1)} %value_hbm.1, ...), custom_call_target="tpu_custom_call" | custom-call | tf_op jit(solution)/shard_map/pallas_call | solution.py:539
  82.9 0.7 broadcast_select_fusion
  (1 shorter events, 0.0 us)

commit v5 on v4

--- a/solution.py
+++ b/solution.py
@@ -50,7 +50,8 @@
 
 
 def kernel(
-    length_ref,
+    length_hbm,
+    question_hbm,
     hidden_hbm,
     attn_gain_hbm,
     ffn_gain_hbm,
@@ -62,6 +63,8 @@
     wup_hbm,
     wdown_hbm,
     out_ref,
+    length_ref,
+    question_ref,
     hidden,
     attn_gain,
     ffn_gain,
@@ -139,8 +142,23 @@
         wgate_hbm,
         wup_hbm,
         wdown_hbm,
-    )
-    targets = (hidden, attn_gain, wq, key, value, ffn_gain, wout, wgate, wup, wdown)
+        length_hbm,
+        question_hbm,
+    )
+    targets = (
+        hidden,
+        attn_gain,
+        wq,
+        key,
+        value,
+        ffn_gain,
+        wout,
+        wgate,
+        wup,
+        wdown,
+        length_ref,
+        question_ref,
+    )
     loads = [
         pltpu.make_async_copy(source, target, load_sems.at[at])
         for at, (source, target) in enumerate(zip(sources, targets))
@@ -252,6 +270,7 @@
     pass_on(4)
     loads[3].wait()
     loads[4].wait()
+    loads[10].wait()
     lx_src[...] = jnp.full((1, 128), length_ref[0].astype(F32), F32)
     word(4)
     for p, offsets in enumerate(QUERY_OFFSETS):
@@ -465,7 +484,9 @@
     )
     lowered = jnp.dot(activated, wdown[...], preferred_element_type=F32)
     result = residual + tp_sum(lowered, d_all, 22, d_sems)
-    out_ref[...] = result.astype(BF16)
+    loads[11].wait()
+    present = lax.broadcasted_iota(jnp.int32, result.shape, 0) < question_ref[0]
+    out_ref[...] = jnp.where(present, result, 0.0).astype(BF16)
 
 
 def body(
@@ -497,8 +518,9 @@
     chunk = (16, 128)
     row = (1, 128)
     dma = pltpu.SemaphoreType.DMA
-    scratch = [pltpu.VMEM(a.shape, a.dtype) for a in operands]
-    scratch += [dma((len(operands),)), dma((23,)), dma((23,))]
+    scratch = [pltpu.SMEM((1,), jnp.int32)] * 2
+    scratch += [pltpu.VMEM(a.shape, a.dtype) for a in operands]
+    scratch += [dma((2 + len(operands),)), dma((23,)), dma((23,))]
     scratch += [
         pltpu.VMEM((2, NX, 4) + chunk, F32),
         pltpu.VMEM((2, NX - 1, 4) + chunk, F32),
@@ -536,19 +558,16 @@
         dma((NT,)),
         dma((NT,)),
     ]
-    result = pl.pallas_call(
+    return pl.pallas_call(
         kernel,
         out_shape=pltpu.VMEM(hidden_in.shape, BF16),
-        in_specs=[pl.BlockSpec(memory_space=pltpu.SMEM)]
-        + [pl.BlockSpec(memory_space=pl.ANY)] * len(operands),
+        in_specs=[pl.BlockSpec(memory_space=pl.ANY)] * (2 + len(operands)),
         out_specs=pl.BlockSpec(memory_space=pltpu.VMEM),
         scratch_shapes=scratch,
         compiler_params=pltpu.CompilerParams(
             collective_id=0, has_side_effects=True, vmem_limit_bytes=60 * 1024 * 1024
         ),
-    )(block_lengths, *operands)
-    present = jnp.arange(ROWS)[:, None] < question_length[0]
-    return jnp.where(present, result, jnp.zeros_like(result))
+    )(block_lengths, question_length, *operands)
 
 
 def solution(mesh):

time: 83.8 us -> 83.5 us (level)
  no operation moved by 1% of the time
where the time goes in v5:
time: 83.5 us; the launch traced here: 83.3 us
  Pallas kernels  81.4 us (97%)
  between operations  1.3 us (2%)
    pallas_call x1, Pallas kernels, body(): pl.pallas_call(kernel, out_shape=pltpu.VMEM(hidden_in.shape, BF16), in_sp...  81.4 us

profile of v5, /device:TPU:1, one launch (start us, length us, event | category | flops | bytes accessed | tf_op | source)
XLA Modules:
  0.0 83.3 jit_solution(4969902731645976655)
XLA Ops:
  1.3 81.4 %shard_map.118 = bf16[64,128]{1,0:T(8,128)(2,1)S(1)} custom-call(s32[1]{0:T(128)S(6)} %copy.15.length_hbm, s32[1]{0:T(128)S(6)} %copy.16.question_hbm, bf16[64,128]{1,0:T(8,128)(2,1)} %hidden_hbm.1, f32[1,128]{1,0:T(1,128)} %bitcast.2, f32[1,128]{1,0:T(1,128)} %bitcast.3, bf16[128,1024]{1,0:T(8,128)(2,1)} %wq_hbm.1, bf16[512,128]{1,0:T(8,128)(2,1)} %key_hbm.1, ...), custom_call_target="tpu_custom_call" | custom-call | tf_op jit(solution)/shard_map/pallas_call | solution.py:561
  82.7 0.6 copy.14
